TPU v7x, 32 devices: a whole 2x2x4 slice. The times are simulated.
32 devices in a mesh: dp: 4 (over z), expert: 2 (over x), head: 4 (over y, core).
Axes of the slice: x: 2, y: 2, z: 4, core: 2. Of those that a mesh axis runs over, the one named last changes fastest.
Arguments:
- hidden_in: bfloat16 [1024, 7168], P(('dp', 'expert'), 'head'), may hold values from -6 to 6
- grad_out: bfloat16 [1024, 7168], P(('dp', 'expert'), 'head'), may hold values from -6 to 6
- expert_ids: int32 [1024, 8], P(('dp', 'expert')), may hold values from 0 to 255, all different within a row; in each aligned block of 128 rows (0 to 127, 128 to 255, ...) at most 8 rows name the same one
- gate_weights: float32 [1024, 8], P(('dp', 'expert')), may hold values from 0.1 to 1
- w_gate: bfloat16 [8, 7168, 2048], P(('dp', 'expert'), None, 'head'), may hold values from -0.0625 to 0.0625
- w_up: bfloat16 [8, 7168, 2048], P(('dp', 'expert'), None, 'head'), may hold values from -0.0625 to 0.0625
- w_down: bfloat16 [8, 2048, 7168], P(('dp', 'expert'), 'head'), may hold values from -0.125 to 0.125
- latent_kv: bfloat16 [1024, 576], P(('dp', 'expert')), may hold values from -16 to 16
- query: bfloat16 [1024, 12288], P('dp', ('expert', 'head')), may hold values from -240 to 240
- d_attn: bfloat16 [1024, 8192], P('dp', ('expert', 'head')), may hold values from -6 to 6
- w_uk: bfloat16 [512, 8192], P(None, ('expert', 'head')), may hold values from -0.25 to 0.25
- w_uv: bfloat16 [512, 8192], P(None, ('expert', 'head')), may hold values from -0.25 to 0.25
- doc_ids: int32 [1024], P('dp'), may hold values from 0 to 15, never falling along the last dimension, each value on 1 to 256 neighbouring positions
Outputs:
- d_hidden: bfloat16 [1024, 7168], P(('dp', 'expert'), 'head')
- d_gates: bfloat16 [1024, 8], P(('dp', 'expert'))
- d_query: bfloat16 [1024, 12288], P('dp', ('expert', 'head'))
- d_latent_kv: bfloat16 [1024, 576], P(('dp', 'expert'), 'head')
Inputs may be any that keep to these rules, and one draw needn't show every extreme that they name: `expert_ids`: each row names 8 different experts; in each aligned block of 128 rows (the rows of one device) no expert is named by more than 8 rows, a bound that some block reaches. `doc_ids`: document numbers never fall; each document has 1 to 256 tokens.
All inputs are finite; a program needn't handle non-finite values.
Results may differ from a plain program's by a relative error of at most 0.0089.
Values may be sent and summed in bfloat16 or wider, within the bound.
A program may use at most 128 MiB of HBM per device.

v0:
```python
import math

import jax
import jax.numpy as jnp
from jax import lax
from jax.sharding import PartitionSpec as P

TOP = 8
LAT = 512
NOPE = 128
ROPE = 64
VD = 128
CAP = 8


CONTRACT_LAST = (((1,), (1,)), ((), ()))


def expert_backward(rows_x, rows_dy, gate_mat, up_mat, down_mat):
    gate_pre = jnp.dot(rows_x, gate_mat, preferred_element_type=jnp.float32)
    up_pre = jnp.dot(rows_x, up_mat, preferred_element_type=jnp.float32)
    back_hidden = lax.dot_general(
        rows_dy, down_mat, CONTRACT_LAST, preferred_element_type=jnp.float32
    )
    sig_val = jax.nn.sigmoid(gate_pre)
    act_val = gate_pre * sig_val
    gate_part = jnp.sum(act_val * up_pre * back_hidden, axis=1)
    d_up = (back_hidden * act_val).astype(jnp.bfloat16)
    d_pre = (back_hidden * up_pre * sig_val * (1.0 + gate_pre * (1.0 - sig_val))).astype(
        jnp.bfloat16
    )
    row_part = lax.dot_general(
        d_pre, gate_mat, CONTRACT_LAST, preferred_element_type=jnp.float32
    ) + lax.dot_general(d_up, up_mat, CONTRACT_LAST, preferred_element_type=jnp.float32)
    return (row_part, gate_part)


def expert_half(hidden_in, grad_out, expert_ids, gate_weights, w_gate, w_up, w_down):
    window_size = lax.axis_size("dp") * lax.axis_size("expert")
    head_count = lax.axis_size("head")
    tok_local = expert_ids.shape[0]
    route_count = tok_local * TOP
    flat_ids = expert_ids.reshape(route_count)
    inside = flat_ids < window_size
    one_hot = (flat_ids[:, None] == jnp.arange(window_size, dtype=jnp.int32)[None, :]).astype(
        jnp.int32
    )
    earlier = jnp.cumsum(one_hot, axis=0) - one_hot
    slot_num = jnp.sum(earlier * one_hot, axis=1)
    target = jnp.where(inside, flat_ids * CAP + slot_num, window_size * CAP)
    slot_hits = target[None, :] == jnp.arange(window_size * CAP, dtype=jnp.int32)[:, None]
    filled = jnp.any(slot_hits, axis=1)
    route_of_slot = jnp.sum(
        jnp.where(slot_hits, jnp.arange(route_count, dtype=jnp.int32)[None, :], 0), axis=1
    )
    token_of_slot = route_of_slot // TOP
    rows_x, rows_dy = (hidden_in, grad_out)
    send_x = jnp.where(filled[:, None], jnp.take(rows_x, token_of_slot, axis=0), 0)
    send_dy = jnp.where(filled[:, None], jnp.take(rows_dy, token_of_slot, axis=0), 0)
    send_x = send_x.reshape(window_size, CAP, send_x.shape[1])
    send_dy = send_dy.reshape(window_size, CAP, send_dy.shape[1])
    got_x = lax.all_to_all(send_x, ("dp", "expert"), split_axis=0, concat_axis=0, tiled=True)
    got_dy = lax.all_to_all(send_dy, ("dp", "expert"), split_axis=0, concat_axis=0, tiled=True)
    got_x, got_dy = (
        lax.all_gather(got_x, "head", axis=2, tiled=True),
        lax.all_gather(got_dy, "head", axis=2, tiled=True),
    )
    sources = got_x.shape[0]
    items = got_x.shape[1]
    flat_x = got_x.reshape(sources * items, got_x.shape[2])
    flat_dy = got_dy.reshape(sources * items, got_dy.shape[2])
    row_part, gate_part = expert_backward(flat_x, flat_dy, w_gate[0], w_up[0], w_down[0])
    gate_spread = jnp.broadcast_to(gate_part[:, None], (sources * items, head_count))
    summed = lax.psum_scatter(row_part, "head", scatter_dimension=1, tiled=True)
    gate_sum = lax.psum_scatter(gate_spread, "head", scatter_dimension=1, tiled=True)
    back_rows = summed.astype(jnp.bfloat16).reshape(sources, items, summed.shape[1])
    back_gate = gate_sum[:, 0].astype(jnp.bfloat16).reshape(sources, items)
    back_rows, back_gate = (
        lax.all_to_all(back_rows, ("dp", "expert"), split_axis=0, concat_axis=0, tiled=True),
        lax.all_to_all(back_gate, ("dp", "expert"), split_axis=0, concat_axis=0, tiled=True),
    )
    flat_back = back_rows.reshape(window_size * CAP, back_rows.shape[2])
    flat_gate = back_gate.reshape(window_size * CAP)
    safe_target = jnp.where(inside, target, 0)
    route_weight = jnp.where(inside, gate_weights.reshape(route_count), 0.0)
    picked = jnp.take(flat_back, safe_target, axis=0).astype(jnp.float32) * route_weight[:, None]
    d_hidden = jnp.sum(picked.reshape(tok_local, TOP, picked.shape[1]), axis=1).astype(jnp.bfloat16)
    d_gates = jnp.where(inside, jnp.take(flat_gate, safe_target), jnp.zeros((), jnp.bfloat16))
    return (d_hidden, d_gates.reshape(tok_local, TOP))


def attention_half(latent_kv, query, d_attn, w_uk, w_uv, doc_ids):
    seq_len = query.shape[0]
    heads_here = w_uk.shape[1] // NOPE
    score_scale = 1.0 / math.sqrt(NOPE + ROPE)
    w_both = jnp.concatenate([w_uk, w_uv], axis=1)
    piece = lax.all_gather(latent_kv, "expert", axis=0, tiled=True)
    lifted = jnp.dot(piece[:, :LAT], w_both, preferred_element_type=jnp.float32).astype(
        jnp.bfloat16
    )
    keyvals = jnp.concatenate([lifted, piece[:, LAT:]], axis=1)
    key_nope = keyvals[:, : heads_here * NOPE].reshape(seq_len, heads_here, NOPE)
    all_values = keyvals[:, heads_here * NOPE : heads_here * (NOPE + VD)].reshape(
        seq_len, heads_here, VD
    )
    rope_key = keyvals[:, heads_here * (NOPE + VD) :]
    all_keys = jnp.concatenate(
        [key_nope, jnp.broadcast_to(rope_key[:, None, :], (seq_len, heads_here, ROPE))], axis=2
    )
    queries = query.reshape(seq_len, heads_here, NOPE + ROPE)
    douts = d_attn.reshape(seq_len, heads_here, VD)
    positions = jnp.arange(seq_len, dtype=jnp.int32)
    block_rows = min(512, seq_len)
    dkey_sum = jnp.zeros((seq_len, heads_here, NOPE + ROPE), jnp.float32)
    dval_sum = jnp.zeros((seq_len, heads_here, VD), jnp.float32)
    dq_blocks = []
    for block_num in range(seq_len // block_rows):
        first_row = block_num * block_rows
        query_blk = queries[first_row : first_row + block_rows]
        dout_blk = douts[first_row : first_row + block_rows]
        scores = (
            jnp.einsum("qhd,khd->hqk", query_blk, all_keys, preferred_element_type=jnp.float32)
            * score_scale
        )
        allowed = (positions[None, :] <= positions[first_row : first_row + block_rows, None]) & (
            doc_ids[None, :] == doc_ids[first_row : first_row + block_rows, None]
        )
        scores = jnp.where(allowed[None], scores, -1e30)
        top_score = jnp.max(scores, axis=2, keepdims=True)
        expd = jnp.exp(scores - top_score)
        probs = expd / jnp.sum(expd, axis=2, keepdims=True)
        dprobs = jnp.einsum(
            "qhd,khd->hqk", dout_blk, all_values, preferred_element_type=jnp.float32
        )
        inner = jnp.sum(probs * dprobs, axis=2, keepdims=True)
        dscore = (probs * (dprobs - inner) * score_scale).astype(jnp.bfloat16)
        prob_low = probs.astype(jnp.bfloat16)
        dq_blocks.append(
            jnp.einsum("hqk,khd->qhd", dscore, all_keys, preferred_element_type=jnp.float32).astype(
                jnp.bfloat16
            )
        )
        dkey_sum = dkey_sum + jnp.einsum(
            "hqk,qhd->khd", dscore, query_blk, preferred_element_type=jnp.float32
        )
        dval_sum = dval_sum + jnp.einsum(
            "hqk,qhd->khd", prob_low, dout_blk, preferred_element_type=jnp.float32
        )
    d_query = jnp.concatenate(dq_blocks, axis=0).reshape(seq_len, heads_here * (NOPE + ROPE))
    dkey_low = dkey_sum.astype(jnp.bfloat16)
    dval_low = dval_sum.astype(jnp.bfloat16)
    row_count = lax.axis_size("expert") * latent_kv.shape[0]
    nope_flat = dkey_low[:, :, :NOPE].reshape(row_count, heads_here * NOPE)
    lat_term = lax.dot_general(
        nope_flat, w_uk, CONTRACT_LAST, preferred_element_type=jnp.float32
    ) + lax.dot_general(
        dval_low.reshape(row_count, heads_here * VD),
        w_uv,
        CONTRACT_LAST,
        preferred_element_type=jnp.float32,
    )
    rope_term = jnp.sum(dkey_low[:, :, NOPE:].astype(jnp.float32), axis=1)
    own_rows = lax.psum_scatter(
        jnp.concatenate([lat_term, rope_term], axis=1), "expert", scatter_dimension=0, tiled=True
    )
    d_latent = lax.psum_scatter(own_rows, "head", scatter_dimension=1, tiled=True)
    return (d_query, d_latent.astype(jnp.bfloat16))


def body(
    hidden_in,
    grad_out,
    expert_ids,
    gate_weights,
    w_gate,
    w_up,
    w_down,
    latent_kv,
    query,
    d_attn,
    w_uk,
    w_uv,
    doc_ids,
):
    d_query, d_latent_kv = attention_half(latent_kv, query, d_attn, w_uk, w_uv, doc_ids)
    d_hidden, d_gates = expert_half(
        hidden_in, grad_out, expert_ids, gate_weights, w_gate, w_up, w_down
    )
    return (d_hidden, d_gates, d_query, d_latent_kv)


def solution(mesh):
    placed = (
        P(("dp", "expert"), "head"),
        P(("dp", "expert"), "head"),
        P(("dp", "expert"), None),
        P(("dp", "expert"), None),
        P(("dp", "expert"), None, "head"),
        P(("dp", "expert"), None, "head"),
        P(("dp", "expert"), "head", None),
        P(("dp", "expert"), None),
        P("dp", ("expert", "head")),
        P("dp", ("expert", "head")),
        P(None, ("expert", "head")),
        P(None, ("expert", "head")),
        P("dp"),
    )
    return jax.shard_map(
        body,
        mesh=mesh,
        in_specs=placed,
        out_specs=(
            P(("dp", "expert"), "head"),
            P(("dp", "expert"), None),
            P("dp", ("expert", "head")),
            P(("dp", "expert"), "head"),
        ),
        check_vma=False,
    )
```

profile of v0, /device:TPU:0, one launch (start us, length us, event | category | flops | bytes accessed | tf_op | source)
XLA Modules:
  0.0 199.1 jit_solution(16776576463837883362)
XLA Ops:
  8.3 2.3 %reduce-window.6 = s32[8,8,128]{2,1,0:T(8,128)S(1)} reduce-window(s32[8,8,128]{2,1,0:T(8,128)S(1)} %fusion.39, s32[]{:T(128)} %constant.44.clone.1), window={size=1x1x128 pad=0_0x0_0x127_0}, to_apply=%region_0.1 | reduce-window | flops 1040384 | bytes 65540 | tf_op jit(solution)/shard_map/reduce-window
  13.8 7.3 %all-to-all-start.1 = ((bf16[8,8,1792]{2,1,0:T(8,128)(2,1)}), bf16[8,8,1792]{2,1,0:T(8,128)(2,1)S(1)}, u32[]{:S(2)}, u32[]{:S(2)}) async-start(bf16[8,8,1792]{2,1,0:T(8,128)(2,1)} %get-tuple-element.34), calls=%async_computation.1 | async-start | bytes 458752 | tf_op jit(solution)/shard_map/all_to_all | solution.py:62
  21.3 7.8 %all_gather.11 = bf16[256,576]{0,1:T(8,128)(2,1)S(1)} all-gather(bf16[128,576]{0,1:T(8,128)(2,1)S(1)} %copy-done.5), channel_id=1, replica_groups=mesh['dp'=4,'expert'=2,'head'=4] {'expert'}, dimensions={0}, use_global_device_ids=true | all-gather | bytes 442368 | tf_op jit(solution)/shard_map/all_gather | solution.py:97
  29.1 1.4 copy.106
  30.5 2.0 fusion.11
  34.0 1.2 copy.88
  35.1 1.5 fusion.61
  37.4 3.6 %fusion.60 = (f32[8,256]{1,0:T(8,128)S(1)}, f32[8,256,256]{1,2,0:T(8,128)}) fusion(pred[256,256]{0,1:T(8,128)(4,1)S(1)} %fusion.31, bf16[256,8,192]{0,2,1:T(8,128)(2,1)} %bitcast.185, bf16[256,8,64]{0,2,1:T(8,128)(2,1)} %broadcast_in_dim.128, bf16[256,8,128]{0,2,1:T(8,128)(2,1)} %bitcast.188), kind=kOutput, calls=%fused_computation.174 | convolution fusion | flops 204996864 | bytes 3743744 | tf_op jit(solution)/shard_map/sub | solution.py:130
  41.0 2.9 %convolution_convert_fusion.3 = bf16[8,256,128]{1,2,0:T(8,128)(2,1)} fusion(bf16[256,8,128]{0,2,1:T(8,128)(2,1)S(1)} %bitcast.180, f32[8,256,256]{1,2,0:T(8,128)} %get-tuple-element.102, f32[8,256]{1,0:T(8,128)S(1)} %get-tuple-element.101), kind=kOutput, calls=%fused_computation.32 | convolution fusion | flops 135528448 | bytes 3153920 | tf_op jit(solution)/shard_map/hqk,qhd->khd/dot_general | solution.py:146
  43.9 4.2 %fusion.19 = bf16[256,8,192]{0,2,1:T(8,128)(2,1)} fusion(bf16[256,8,192]{0,2,1:T(8,128)(2,1)} %bitcast.186, f32[8,256,256]{2,1,0:T(8,128)S(1)} %fusion.61, f32[8,256,256]{1,2,0:T(8,128)} %get-tuple-element.102, f32[8,256]{1,0:T(8,128)S(1)} %get-tuple-element.101), kind=kOutput, calls=%fused_computation.33 | convolution fusion | flops 205392128 | bytes 5775360 | tf_op jit(solution)/shard_map/hqk,qhd->khd/dot_general | solution.py:143
  48.1 1.6 convert_reduce_fusion
  50.8 1.7 fusion.62
  53.4 1.9 convolution_add_fusion.1
  56.2 4.8 %all-to-all-start = ((bf16[8,8,1792]{2,1,0:T(8,128)(2,1)}), bf16[8,8,1792]{2,1,0:T(8,128)(2,1)S(1)}, u32[]{:S(2)}, u32[]{:S(2)}) async-start(bf16[8,8,1792]{2,1,0:T(8,128)(2,1)} %get-tuple-element.33), calls=%async_computation | async-start | bytes 458752 | tf_op jit(solution)/shard_map/all_to_all | solution.py:63
  61.1 9.5 %all_gather.10 = bf16[8,8,7168]{2,1,0:T(8,128)(2,1)S(1)} all-gather(bf16[8,8,1792]{2,1,0:T(8,128)(2,1)S(1)} %all-to-all-done.1), channel_id=1, replica_groups=mesh['dp'=4,'expert'=2,'head'=4] {'head'}, dimensions={2}, use_global_device_ids=true | all-gather | bytes 1146880 | tf_op jit(solution)/shard_map/all_gather | solution.py:65
  70.5 4.6 %fusion.4 = f32[64,512]{1,0:T(8,128)S(1)} fusion(bf16[1,7168,512]{2,1,0:T(8,128)(2,1)} %param.19, bf16[8,8,7168]{2,1,0:T(8,128)(2,1)S(1)} %all_gather.10), kind=kOutput, calls=%fused_computation.8 | convolution fusion | flops 469762048 | bytes 8388608 | tf_op jit(solution)/shard_map/dot_general | solution.py:20
  75.2 1.4 fusion.7
  76.6 9.6 %all_gather.9 = bf16[8,8,7168]{2,1,0:T(8,128)(2,1)S(1)} all-gather(bf16[8,8,1792]{2,1,0:T(8,128)(2,1)S(1)} %all-to-all-done), channel_id=1, replica_groups=mesh['dp'=4,'expert'=2,'head'=4] {'head'}, dimensions={2}, use_global_device_ids=true | all-gather | bytes 1146880 | tf_op jit(solution)/shard_map/all_gather | solution.py:66
  86.2 5.7 %multiply_reduce_fusion.1 = (f32[64]{0:T(128)S(1)}, f32[64,512]{1,0:T(8,128)S(1)}) fusion(f32[64,512]{1,0:T(8,128)S(1)} %fusion.7, f32[64,512]{1,0:T(8,128)S(1)} %fusion.4, bf16[1,512,7168]{2,1,0:T(8,128)(2,1)} %param.21, bf16[8,8,7168]{2,1,0:T(8,128)(2,1)S(1)} %all_gather.9), kind=kOutput, calls=%fused_computation.60 | convolution fusion | flops 469991360 | bytes 8651008 | tf_op jit(solution)/shard_map/dot_general | solution.py:22
  91.9 5.5 %fusion.2 = f32[64,7168]{1,0:T(8,128)S(1)} fusion(bf16[1,7168,512]{2,1,0:T(8,128)(2,1)} %param.19, f32[64,512]{1,0:T(8,128)S(1)} %fusion.4, f32[64,512]{1,0:T(8,128)S(1)} %get-tuple-element.100, f32[64,512]{1,0:T(8,128)S(1)} %fusion.7), kind=kOutput, calls=%fused_computation.6 | convolution fusion | flops 470089728 | bytes 9568256 | tf_op jit(solution)/shard_map/dot_general | solution.py:32
  97.5 3.6 %convolution_add_fusion = f32[64,7168]{1,0:T(8,128)} fusion(f32[64,7168]{1,0:T(8,128)S(1)} %fusion.2, bf16[1,7168,512]{2,1,0:T(8,128)(2,1)S(1)} %bitcast.178, f32[64,512]{1,0:T(8,128)S(1)} %get-tuple-element.100, f32[64,512]{1,0:T(8,128)S(1)} %fusion.4), kind=kOutput, calls=%fused_computation.5 | convolution fusion | flops 470417408 | bytes 11272192 | tf_op jit(solution)/shard_map/dot_general | solution.py:34
  102.3 3.3 %convolution_convert_fusion.2 = bf16[8,192,256]{2,1,0:T(8,128)(2,1)S(1)} fusion(f32[8,256,256]{2,1,0:T(8,128)S(1)} %fusion.61, bf16[256,8,64]{0,2,1:T(8,128)(2,1)} %broadcast_in_dim.128, bf16[256,8,128]{0,2,1:T(8,128)(2,1)} %bitcast.189, f32[8,256,256]{1,2,0:T(8,128)} %get-tuple-element.102, f32[8,256]{1,0:T(8,128)S(1)} %get-tuple-element.101), kind=kOutput, calls=%fused_computation.31 | convolution fusion | flops 206964992 | bytes 5775360 | tf_op jit(solution)/shard_map/hqk,khd->qhd/dot_general | solution.py:139
  105.7 6.4 %all-reduce = bf16[64,4]{0,1:T(4,128)(2,1)S(1)} all-reduce(f32[64,4]{0,1:T(4,128)S(1)} %broadcast_in_dim.125), channel_id=3, replica_groups=mesh['dp'=4,'expert'=2,'head'=4] {'head'}, use_global_device_ids=true, to_apply=%region_8.10.clone | all-reduce | flops 256 | bytes 1536
  113.5 5.7 %all-to-all-start.3 = ((bf16[8,1,8]{2,1,0:T(2,128)(2,1)}), bf16[8,1,8]{2,1,0:T(2,128)(2,1)S(1)}, u32[]{:S(2)}, u32[]{:S(2)}) async-start(bf16[8,1,8]{2,1,0:T(2,128)(2,1)} %convert_element_type.97), calls=%async_computation.4 | async-start | bytes 8192 | tf_op jit(solution)/shard_map/all_to_all | solution.py:80
  119.3 1.2 copy.98
  120.4 5.1 %all-to-all-done.3 = bf16[8,1,8]{2,1,0:T(2,128)(2,1)S(1)} async-done(((bf16[8,1,8]{2,1,0:T(2,128)(2,1)}), bf16[8,1,8]{2,1,0:T(2,128)(2,1)S(1)}, u32[]{:S(2)}, u32[]{:S(2)}) %all-to-all-start.3) | async-done | bytes 160 | tf_op jit(solution)/shard_map/all_to_all | solution.py:80
  128.5 1.8 copy.104
  131.5 1.7 convert_bitcast_fusion
  133.3 5.5 %all-to-all-start.2 = ((bf16[8,8,1792]{2,1,0:T(8,128)(2,1)}), bf16[8,8,1792]{2,1,0:T(8,128)(2,1)S(1)}, u32[]{:S(2)}, u32[]{:S(2)}) async-start(bf16[8,8,1792]{2,1,0:T(8,128)(2,1)} %convert_bitcast_fusion), calls=%async_computation.3 | async-start | bytes 458752 | tf_op jit(solution)/shard_map/all_to_all | solution.py:79
  138.8 39.9 %compare_select_fusion.2 = bf16[1024]{0:T(1024)(128)(2,1)S(1)} fusion(s32[1024]{0:T(1024)S(1)} %bitcast.193, bf16[]{:T(256)} %bitcast.13, bf16[]{:T(256)} %bitcast.14, bf16[]{:T(256)} %bitcast.15, bf16[]{:T(256)} %bitcast.16, bf16[]{:T(256)} %bitcast.17, bf16[]{:T(256)} %bitcast.18, bf16[]{:T(256)} %bitcast.19, bf16[]{:T(256)} %bitcast.20, bf16[]{:T(256)} %bitcast.21, ...), kind=kLoop, calls=%fused_computation.85 | loop fusion | flops 129024 | bytes 6272 | tf_op jit(solution)/shard_map/jit(_take)/gather | solution.py:88
  181.2 5.8 %gather_fusion = bf16[1024,1792]{1,0:T(8,128)(2,1)} fusion(bf16[64,1792]{1,0:T(8,128)(2,1)S(1)} %bitcast.174, s32[1024]{0:T(1024)S(1)} %broadcast_clamp_fusion), kind=kCustom, calls=%fused_computation.2 | custom fusion | bytes 7344128 | tf_op jit(solution)/shard_map/jit(_take)/gather | solution.py:86
  187.0 5.6 %multiply_reduce_fusion = bf16[128,1792]{1,0:T(8,128)(2,1)} fusion(bf16[1024,1792]{1,0:T(8,128)(2,1)} %gather_fusion, f32[128,8]{1,0:T(8,128)S(1)} %get-tuple-element.27, pred[128,8]{1,0:T(8,128)(4,1)S(1)} %get-tuple-element.26), kind=kLoop, calls=%fused_computation.15 | loop fusion | flops 7110656 | bytes 4133888 | tf_op jit(solution)/shard_map/reduce_sum | solution.py:87
  (87 shorter events, 19.0 us)
Async XLA Ops:
  7.2 4.2 %copy-start = (bf16[128,1792]{1,0:T(8,128)(2,1)S(1)}, bf16[128,1792]{1,0:T(8,128)(2,1)}, u32[]{:S(2)}) copy-start(bf16[128,1792]{1,0:T(8,128)(2,1)} %param.15) | copy-start | bytes 1376260
  7.2 5.0 %copy-start.1 = (bf16[128,1792]{1,0:T(8,128)(2,1)S(1)}, bf16[128,1792]{1,0:T(8,128)(2,1)}, u32[]{:S(2)}) copy-start(bf16[128,1792]{1,0:T(8,128)(2,1)} %param.16) | copy-start | bytes 1376260
  12.2 9.0 %copy-start.7 = (s32[256]{0:T(256)S(1)}, s32[256]{0:T(256)}, u32[]{:S(2)}) copy-start(s32[256]{0:T(256)} %param.27) | copy-start | bytes 3076
  12.2 9.1 %copy-start.5 = (bf16[128,576]{0,1:T(8,128)(2,1)S(1)}, bf16[128,576]{0,1:T(8,128)(2,1)}, u32[]{:S(2)}) copy-start(bf16[128,576]{0,1:T(8,128)(2,1)} %param.22) | copy-start | bytes 442372
  12.2 18.3 %copy-start.2 = (bf16[512,1024]{1,0:T(8,128)(2,1)S(1)}, bf16[512,1024]{1,0:T(8,128)(2,1)}, u32[]{:S(2)}) copy-start(bf16[512,1024]{1,0:T(8,128)(2,1)} %param.25) | copy-start | bytes 3145732
  13.8 42.4 %all-to-all-start.1 = ((bf16[8,8,1792]{2,1,0:T(8,128)(2,1)}), bf16[8,8,1792]{2,1,0:T(8,128)(2,1)S(1)}, u32[]{:S(2)}, u32[]{:S(2)}) async-start(bf16[8,8,1792]{2,1,0:T(8,128)(2,1)} %get-tuple-element.34), calls=%async_computation.1 | async-start | bytes 458752 | tf_op jit(solution)/shard_map/all_to_all | solution.py:62
  21.1 107.4 %reduce-scatter.8.cloned.1.call-start = ((), (), s32[]{:S(2)}) async-start(), calls=%async_computation.8 | async-start | bytes 983040 | tf_op jit(solution)/shard_map/reduce_scatter | solution.py:163
  29.1 1.4 copy-start.4
  32.5 1.5 copy-start.3
  34.0 2.7 %slice-start.4 = ((bf16[256,576]{0,1:T(8,128)(2,1)}), bf16[256,64]{0,1:T(8,128)(2,1)S(1)}, s32[]{:S(2)}) async-start(bf16[256,576]{0,1:T(8,128)(2,1)} %copy-done.4), calls=%async_computation.14 | async-start | bytes 65536 | tf_op jit(solution)/shard_map/slice | solution.py:101
  56.2 20.4 %all-to-all-start = ((bf16[8,8,1792]{2,1,0:T(8,128)(2,1)}), bf16[8,8,1792]{2,1,0:T(8,128)(2,1)S(1)}, u32[]{:S(2)}, u32[]{:S(2)}) async-start(bf16[8,8,1792]{2,1,0:T(8,128)(2,1)} %get-tuple-element.33), calls=%async_computation | async-start | bytes 458752 | tf_op jit(solution)/shard_map/all_to_all | solution.py:63
  61.0 70.5 %reduce-scatter.6.cloned.1.call-start = ((), (), s32[]{:S(2)}) async-start(), calls=%async_computation.7 | async-start | bytes 2293760 | tf_op jit(solution)/shard_map/reduce_scatter | solution.py:74
  61.1 14.1 %slice-start = ((s8[7340032]{0:T(1024)(128)(4,1)}), s8[4194304]{0:T(1024)(128)(4,1)S(1)}, s32[]{:S(2)}) async-start(s8[7340032]{0:T(1024)(128)(4,1)} %bitcast.175), calls=%async_computation.10 | async-start | bytes 8388608
  70.5 4.7 %slice-start.1 = ((s8[7340032]{0:T(1024)(128)(4,1)}), s8[3145728]{0:T(1024)(128)(4,1)S(1)}, s32[]{:S(2)}) async-start(s8[7340032]{0:T(1024)(128)(4,1)} %bitcast.175), calls=%async_computation.11 | async-start | bytes 6291456
  86.2 11.3 %slice-start.2 = ((s8[7340032]{0:T(1024)(128)(4,1)}), s8[4194304]{0:T(1024)(128)(4,1)S(1)}, s32[]{:S(2)}) async-start(s8[7340032]{0:T(1024)(128)(4,1)} %bitcast.177), calls=%async_computation.12 | async-start | bytes 8388608
  91.9 5.6 %slice-start.3 = ((s8[7340032]{0:T(1024)(128)(4,1)}), s8[3145728]{0:T(1024)(128)(4,1)S(1)}, s32[]{:S(2)}) async-start(s8[7340032]{0:T(1024)(128)(4,1)} %bitcast.177), calls=%async_computation.13 | async-start | bytes 6291456
  97.5 3.7 %copy-start.6 = (f32[128,8]{0,1:T(8,128)S(1)}, f32[128,8]{0,1:T(8,128)}, u32[]{:S(2)}) copy-start(f32[128,8]{0,1:T(8,128)} %param.18) | copy-start | bytes 12292
  101.1 0.7 copy-start.8
  113.5 12.1 %all-to-all-start.3 = ((bf16[8,1,8]{2,1,0:T(2,128)(2,1)}), bf16[8,1,8]{2,1,0:T(2,128)(2,1)S(1)}, u32[]{:S(2)}, u32[]{:S(2)}) async-start(bf16[8,1,8]{2,1,0:T(2,128)(2,1)} %convert_element_type.97), calls=%async_computation.4 | async-start | bytes 8192 | tf_op jit(solution)/shard_map/all_to_all | solution.py:80
  119.1 60.3 %reduce-scatter.10.cloned.1.call-start = ((), (), s32[]{:S(2)}) async-start(), calls=%async_computation.9 | async-start | bytes 368640
  133.3 47.9 %all-to-all-start.2 = ((bf16[8,8,1792]{2,1,0:T(8,128)(2,1)}), bf16[8,8,1792]{2,1,0:T(8,128)(2,1)S(1)}, u32[]{:S(2)}, u32[]{:S(2)}) async-start(bf16[8,8,1792]{2,1,0:T(8,128)(2,1)} %convert_bitcast_fusion), calls=%async_computation.3 | async-start | bytes 458752 | tf_op jit(solution)/shard_map/all_to_all | solution.py:79
Sparse Core Ops, SparseCore 0:
  56.3 18.3 reduce-scatter.7
  101.2 30.2 reduce-scatter.5
  134.6 20.2 reduce-scatter.9
where the time goes:
time: 201 us; the launch traced here: 199 us
  other arithmetic  53.6 us (27%)
  matrix products  41.9 us (21%)
  blocking collectives  33.3 us (17%)
  local copies, waits for them, and re-layouts  26.4 us (13%)
  starting transfers between devices  23.3 us (12%)
  between operations  14.2 us (7%)
  waiting for transfers between devices  6.3 us (3%)
    gather x1, other arithmetic, expert_half(): jnp.take(flat_gate, safe_target)  39.9 us
    all_gather x1, blocking collectives, expert_half(): lax.all_gather(got_dy, 'head', axis=2, tiled=True)  9.6 us
    all_gather x1, blocking collectives, expert_half(): lax.all_gather(got_x, 'head', axis=2, tiled=True)  9.47 us
    unnamed x35, local copies, waits for them, and re-layouts  8.81 us
    all_gather x1, blocking collectives, attention_half(): piece = lax.all_gather(latent_kv, 'expert', axis=0, tiled=True)  7.85 us
    all_to_all x1, starting transfers between devices, expert_half(): lax.all_to_all(send_x, ('dp', 'expert'), split_axis=0, concat_axis=0, til...  7.25 us
    unnamed x1, blocking collectives  6.42 us
    gather x1, local copies, waits for them, and re-layouts, expert_half(): jnp.take(flat_back, safe_target, axis=0).astype(jnp.float32)  5.82 us
  transfers between devices with their start and end apart: 7, of which 2 were waited for; matrix products, arithmetic and copies ran while one was open for 52% of the time, Pallas kernels for 0%

commit v1 on v0

--- a/solution.py
+++ b/solution.py
@@ -35,58 +35,61 @@
     return (row_part, gate_part)
 
 
+def routing(expert_ids, gate_weights, window_size):
+    tok_local = expert_ids.shape[0]
+    names = expert_ids[:, :, None] == jnp.arange(window_size, dtype=jnp.int32)[None, None, :]
+    member = jnp.any(names, axis=1)
+    weight = jnp.sum(jnp.where(names, gate_weights[:, :, None], 0.0), axis=1)
+    before = jnp.tril(jnp.ones((tok_local, tok_local), jnp.bfloat16), -1)
+    earlier = jnp.dot(before, member.astype(jnp.bfloat16), preferred_element_type=jnp.float32)
+    slot_num = jnp.where(member, earlier.astype(jnp.int32), -1)
+    hits = slot_num[:, :, None] == jnp.arange(CAP, dtype=jnp.int32)[None, None, :]
+    slots = window_size * CAP
+    combine = jnp.where(hits, weight[:, :, None], 0.0).reshape(tok_local, slots)
+    hits = hits.reshape(tok_local, slots)
+    return (hits, combine, names)
+
+
 def expert_half(hidden_in, grad_out, expert_ids, gate_weights, w_gate, w_up, w_down):
     window_size = lax.axis_size("dp") * lax.axis_size("expert")
     head_count = lax.axis_size("head")
-    tok_local = expert_ids.shape[0]
-    route_count = tok_local * TOP
-    flat_ids = expert_ids.reshape(route_count)
-    inside = flat_ids < window_size
-    one_hot = (flat_ids[:, None] == jnp.arange(window_size, dtype=jnp.int32)[None, :]).astype(
-        jnp.int32
-    )
-    earlier = jnp.cumsum(one_hot, axis=0) - one_hot
-    slot_num = jnp.sum(earlier * one_hot, axis=1)
-    target = jnp.where(inside, flat_ids * CAP + slot_num, window_size * CAP)
-    slot_hits = target[None, :] == jnp.arange(window_size * CAP, dtype=jnp.int32)[:, None]
-    filled = jnp.any(slot_hits, axis=1)
-    route_of_slot = jnp.sum(
-        jnp.where(slot_hits, jnp.arange(route_count, dtype=jnp.int32)[None, :], 0), axis=1
-    )
-    token_of_slot = route_of_slot // TOP
-    rows_x, rows_dy = (hidden_in, grad_out)
-    send_x = jnp.where(filled[:, None], jnp.take(rows_x, token_of_slot, axis=0), 0)
-    send_dy = jnp.where(filled[:, None], jnp.take(rows_dy, token_of_slot, axis=0), 0)
-    send_x = send_x.reshape(window_size, CAP, send_x.shape[1])
-    send_dy = send_dy.reshape(window_size, CAP, send_dy.shape[1])
-    got_x = lax.all_to_all(send_x, ("dp", "expert"), split_axis=0, concat_axis=0, tiled=True)
-    got_dy = lax.all_to_all(send_dy, ("dp", "expert"), split_axis=0, concat_axis=0, tiled=True)
-    got_x, got_dy = (
-        lax.all_gather(got_x, "head", axis=2, tiled=True),
-        lax.all_gather(got_dy, "head", axis=2, tiled=True),
-    )
-    sources = got_x.shape[0]
-    items = got_x.shape[1]
-    flat_x = got_x.reshape(sources * items, got_x.shape[2])
-    flat_dy = got_dy.reshape(sources * items, got_dy.shape[2])
+    tok_local, width = hidden_in.shape
+    slots = window_size * CAP
+    hits, combine, names = routing(expert_ids, gate_weights, window_size)
+    pick = hits.astype(jnp.bfloat16)
+    rows = jnp.concatenate([hidden_in, grad_out], axis=1)
+    send = lax.dot_general(
+        pick, rows, (((0,), (0,)), ((), ())), preferred_element_type=jnp.float32
+    ).astype(jnp.bfloat16)
+    send = send.reshape(window_size, CAP, 2 * width)
+    got = lax.all_to_all(send, ("dp", "expert"), split_axis=0, concat_axis=0, tiled=True)
+    got = lax.all_gather(got.reshape(slots, 2 * width), "head", axis=0, tiled=False)
+    flat_x = got[:, :, :width].transpose(1, 0, 2).reshape(slots, head_count * width)
+    flat_dy = got[:, :, width:].transpose(1, 0, 2).reshape(slots, head_count * width)
     row_part, gate_part = expert_backward(flat_x, flat_dy, w_gate[0], w_up[0], w_down[0])
-    gate_spread = jnp.broadcast_to(gate_part[:, None], (sources * items, head_count))
-    summed = lax.psum_scatter(row_part, "head", scatter_dimension=1, tiled=True)
-    gate_sum = lax.psum_scatter(gate_spread, "head", scatter_dimension=1, tiled=True)
-    back_rows = summed.astype(jnp.bfloat16).reshape(sources, items, summed.shape[1])
-    back_gate = gate_sum[:, 0].astype(jnp.bfloat16).reshape(sources, items)
-    back_rows, back_gate = (
-        lax.all_to_all(back_rows, ("dp", "expert"), split_axis=0, concat_axis=0, tiled=True),
-        lax.all_to_all(back_gate, ("dp", "expert"), split_axis=0, concat_axis=0, tiled=True),
-    )
-    flat_back = back_rows.reshape(window_size * CAP, back_rows.shape[2])
-    flat_gate = back_gate.reshape(window_size * CAP)
-    safe_target = jnp.where(inside, target, 0)
-    route_weight = jnp.where(inside, gate_weights.reshape(route_count), 0.0)
-    picked = jnp.take(flat_back, safe_target, axis=0).astype(jnp.float32) * route_weight[:, None]
-    d_hidden = jnp.sum(picked.reshape(tok_local, TOP, picked.shape[1]), axis=1).astype(jnp.bfloat16)
-    d_gates = jnp.where(inside, jnp.take(flat_gate, safe_target), jnp.zeros((), jnp.bfloat16))
-    return (d_hidden, d_gates.reshape(tok_local, TOP))
+    parts = row_part.astype(jnp.bfloat16).reshape(slots, head_count, width)
+    gate_cols = jnp.broadcast_to(
+        gate_part.astype(jnp.bfloat16)[:, None, None], (slots, head_count, 128)
+    )
+    parts = jnp.concatenate([parts, gate_cols], axis=2).transpose(1, 0, 2)
+    parts = lax.all_to_all(parts, "head", split_axis=0, concat_axis=0, tiled=True)
+    summed = jnp.sum(parts.astype(jnp.float32), axis=0).astype(jnp.bfloat16)
+    summed = summed.reshape(window_size, CAP, width + 128)
+    back = lax.all_to_all(summed, ("dp", "expert"), split_axis=0, concat_axis=0, tiled=True)
+    back = back.reshape(slots, width + 128)
+    high = combine.astype(jnp.bfloat16)
+    rest = combine - high.astype(jnp.float32)
+    low = rest.astype(jnp.bfloat16)
+    flat_back = back[:, :width]
+    d_hidden = jnp.dot(
+        jnp.concatenate([high, low], axis=1),
+        jnp.concatenate([flat_back, flat_back], axis=0),
+        preferred_element_type=jnp.float32,
+    ).astype(jnp.bfloat16)
+    gate_of = jnp.where(hits, back[:, width].astype(jnp.float32)[None, :], 0.0)
+    gate_of = jnp.sum(gate_of.reshape(tok_local, window_size, CAP), axis=2)
+    d_gates = jnp.sum(jnp.where(names, gate_of[:, None, :], 0.0), axis=2).astype(jnp.bfloat16)
+    return (d_hidden, d_gates)
 
 
 def attention_half(latent_kv, query, d_attn, w_uk, w_uv, doc_ids):

time: 201 us -> 115 us (0.57)
  other arithmetic: 53.6 us -> 5.68 us
  blocking collectives: 33.3 us -> 9.75 us
  waiting for transfers between devices: 6.3 us -> 18.8 us
  local copies, waits for them, and re-layouts: 26.4 us -> 15.4 us
  matrix products: 41.9 us -> 32 us
  starting transfers between devices: 23.3 us -> 16.8 us
    gather x3 -> x0, other arithmetic: 39.9 us -> none  [the longest x1 39.9 us: expert_half(): jnp.take(flat_gate, safe_target)]
    all_gather x2 -> x0, blocking collectives: 19.1 us -> none  [the longest x1 9.6 us: expert_half(): lax.all_gather(got_dy, 'head', axis=2, tiled=True)]
    gather x8 -> x0, local copies, waits for them, and re-layouts: 10.3 us -> none  [the longest x1 5.82 us: expert_half(): jnp.take(flat_back, safe_target, axis=0).astype(jnp.float32)]
    all_to_all x4 -> x3, waiting for transfers between devices: 5.09 us -> 14.1 us  [the longest x1 11.8 us: expert_half(): lax.all_to_all(parts, 'head', split_axis=0, concat_axis=0, tiled=True)]
    all_to_all x4 -> x3, starting transfers between devices: 23.2 us -> 16.7 us  [the longest x1 7.38 us: expert_half(): lax.all_to_all(send, ('dp', 'expert'), split_axis=0, concat_axis=0, tiled...]
    unnamed x1 -> x0, blocking collectives: 6.42 us -> none
    reduce_sum x3, other arithmetic: 5.72 us -> 1.57 us  [the longest x1 0.88 us: expert_half(): summed = jnp.sum(parts.astype(jnp.float32), axis=0).astype(jnp.bfloat16)]
    unnamed x35 -> x50, local copies, waits for them, and re-layouts: 8.81 us -> 12.8 us
  transfers between devices with their start and end apart: 7 -> 6, of which waited for: 2 -> 5; matrix products, arithmetic and copies ran while one was open for 52% -> 36% of each run, Pallas kernels for 0% -> 0%
where the time goes in v1:
time: 115 us; the launch traced here: 114 us
  matrix products  32 us (28%)
  waiting for transfers between devices  18.8 us (16%)
  starting transfers between devices  16.8 us (15%)
  between operations  15.9 us (14%)
  local copies, waits for them, and re-layouts  15.4 us (13%)
  blocking collectives  9.75 us (8%)
  other arithmetic  5.68 us (5%)
    unnamed x50, local copies, waits for them, and re-layouts  12.8 us
    all_to_all x1, waiting for transfers between devices, expert_half(): lax.all_to_all(parts, 'head', split_axis=0, concat_axis=0, tiled=True)  11.8 us
    all_gather x1, blocking collectives, attention_half(): piece = lax.all_gather(latent_kv, 'expert', axis=0, tiled=True)  9.75 us
    all_to_all x1, starting transfers between devices, expert_half(): lax.all_to_all(send, ('dp', 'expert'), split_axis=0, concat_axis=0, tiled...  7.38 us
    all_to_all x1, starting transfers between devices, expert_half(): lax.all_to_all(summed, ('dp', 'expert'), split_axis=0, concat_axis=0, til...  5.67 us
    dot_general x1, matrix products, expert_backward(): gate_pre = jnp.dot(rows_x, gate_mat, preferred_element_type=jnp.float32)  4.6 us
    dot_general x1, matrix products, attention_half(): jnp.einsum('hqk,qhd->khd', dscore, query_blk, preferred_element_type=jnp....  4.51 us
    all_to_all x1, starting transfers between devices, expert_half(): lax.all_to_all(parts, 'head', split_axis=0, concat_axis=0, tiled=True)  3.64 us
  transfers between devices with their start and end apart: 6, of which 5 were waited for; matrix products, arithmetic and copies ran while one was open for 36% of the time, Pallas kernels for 0%

profile of v1, /device:TPU:0, one launch (start us, length us, event | category | flops | bytes accessed | tf_op | source)
XLA Modules:
  0.0 114.3 jit_solution(15773206039133319734)
XLA Ops:
  9.1 2.3 %fusion.12 = bf16[8,8,3584]{2,1,0:T(8,128)(2,1)} fusion(bf16[128,1792]{1,0:T(8,128)(2,1)} %param.14, bf16[128,1792]{1,0:T(8,128)(2,1)} %param.13, s32[64]{0:T(128)S(1)} %eq.62, s32[128,8]{0,1:T(8,128)S(1)} %fusion.22), kind=kOutput, calls=%fused_computation.14 | convolution fusion | flops 60792832 | bytes 1380608 | tf_op jit(solution)/shard_map/dot_general | solution.py:61
  11.4 7.4 %all-to-all-start = ((bf16[8,8,3584]{2,1,0:T(8,128)(2,1)}), bf16[8,8,3584]{2,1,0:T(8,128)(2,1)S(1)}, u32[]{:S(2)}, u32[]{:S(2)}) async-start(bf16[8,8,3584]{2,1,0:T(8,128)(2,1)} %fusion.12), calls=%async_computation | async-start | bytes 917504 | tf_op jit(solution)/shard_map/all_to_all | solution.py:65
  18.9 9.7 %all_gather.7 = bf16[256,576]{0,1:T(8,128)(2,1)S(1)} all-gather(bf16[128,576]{0,1:T(8,128)(2,1)S(1)} %copy-done.11), channel_id=1, replica_groups=mesh['dp'=4,'expert'=2,'head'=4] {'expert'}, dimensions={0}, use_global_device_ids=true | all-gather | bytes 442368 | tf_op jit(solution)/shard_map/all_gather | solution.py:100
  29.6 1.2 %copy.56 = bf16[256,1536]{0,1:T(8,128)(2,1)} copy(bf16[256,1536]{1,0:T(8,128)(2,1)S(1)} %copy-done.3) | data formatting | bytes 1572864 | tf_op args[8]
  30.7 1.2 %all-to-all-done = bf16[8,8,3584]{2,1,0:T(8,128)(2,1)S(1)} async-done(((bf16[8,8,3584]{2,1,0:T(8,128)(2,1)}), bf16[8,8,3584]{2,1,0:T(8,128)(2,1)S(1)}, u32[]{:S(2)}, u32[]{:S(2)}) %all-to-all-start) | async-done | bytes 458784 | tf_op jit(solution)/shard_map/all_to_all | solution.py:65
  32.9 2.0 %fusion.13 = bf16[256,2048]{0,1:T(8,128)(2,1)S(1)} fusion(bf16[512,1024]{1,0:T(8,128)(2,1)} %param.24, bf16[512,1024]{1,0:T(8,128)(2,1)S(1)} %copy-done.1, bf16[256,576]{0,1:T(8,128)(2,1)S(1)} %copy-done.8), kind=kOutput, calls=%fused_computation.16 | convolution fusion | flops 541589504 | bytes 3407872 | tf_op jit(solution)/shard_map/dot_general | solution.py:101
  36.0 2.2 %fusion.72 = (f32[8,256]{1,0:T(8,128)S(1)}, f32[8,256,256]{1,2,0:T(8,128)}) fusion(pred[256,256]{0,1:T(8,128)(4,1)S(1)} %fusion.36, bf16[256,8,192]{0,2,1:T(8,128)(2,1)S(1)} %bitcast.129, bf16[256,8,64]{0,2,1:T(8,128)(2,1)S(1)} %broadcast_in_dim.104, bf16[256,8,128]{0,2,1:T(8,128)(2,1)S(1)} %bitcast.132), kind=kOutput, calls=%fused_computation.105 | convolution fusion | flops 204996864 | bytes 3743744 | tf_op jit(solution)/shard_map/sub | solution.py:133
  38.7 4.5 %fusion.21 = bf16[256,8,192]{0,2,1:T(8,128)(2,1)} fusion(bf16[256,8,192]{0,2,1:T(8,128)(2,1)} %bitcast.128, f32[8,256,256]{2,1,0:T(8,128)S(1)} %fusion.73, f32[8,256,256]{1,2,0:T(8,128)} %get-tuple-element.29, f32[8,256]{1,0:T(8,128)S(1)} %get-tuple-element.28), kind=kOutput, calls=%fused_computation.32 | convolution fusion | flops 205392128 | bytes 5775360 | tf_op jit(solution)/shard_map/hqk,qhd->khd/dot_general | solution.py:146
  43.3 1.1 slice.48
  44.3 1.0 convert_reduce_fusion
  45.4 1.9 %fusion.74 = f32[256,512]{1,0:T(8,128)S(1)} fusion(bf16[256,1024]{0,1:T(8,128)(2,1)S(1)} %bitcast.122, bf16[512,1024]{1,0:T(8,128)(2,1)} %param.23), kind=kOutput, calls=%fused_computation.107 | convolution fusion | flops 268435456 | bytes 2097152 | tf_op jit(solution)/shard_map/dot_general | solution.py:157
  49.1 0.9 pad_maximum_fusion.1
  50.0 3.4 %all-gather.2.cloned.1.call-done = bf16[4,64,3584]{2,1,0:T(8,128)(2,1)} async-done(((bf16[1,64,3584]{2,1,0:T(8,128)(2,1)}), bf16[4,64,3584]{2,1,0:T(8,128)(2,1)}) %all-gather.2.cloned.1.call-update) | async-done | bytes 1835024 | tf_op jit(solution)/shard_map/all_gather | solution.py:66
  53.4 1.6 %slice_bitcast_fusion = (bf16[4,8,8,1792]{3,2,1,0:T(8,128)(2,1)S(1)}, bf16[4,8,8,1792]{3,2,1,0:T(8,128)(2,1)S(1)}) fusion(bf16[4,64,3584]{2,1,0:T(8,128)(2,1)} %all-gather.2.cloned.1.call-done), kind=kLoop, calls=%fused_computation.44 | loop fusion | bytes 3670016
  55.1 4.6 %fusion.5 = f32[64,512]{1,0:T(8,128)S(1)} fusion(bf16[64,7168]{1,0:T(8,128)(2,1)S(1)} %bitcast.113, bf16[1,7168,512]{2,1,0:T(8,128)(2,1)} %param.17), kind=kOutput, calls=%fused_computation.6 | convolution fusion | flops 469762048 | bytes 8388608 | tf_op jit(solution)/shard_map/dot_general | solution.py:20
  60.3 1.4 %fusion.8 = f32[64,512]{1,0:T(8,128)S(1)} fusion(bf16[64,7168]{1,0:T(8,128)(2,1)S(1)} %bitcast.114, bf16[1,7168,512]{2,1,0:T(8,128)(2,1)S(1)} %bitcast.112), kind=kOutput, calls=%fused_computation.9 | convolution fusion | flops 469762048 | bytes 8388608 | tf_op jit(solution)/shard_map/dot_general | solution.py:21
  61.8 2.1 %slice-done.5 = s8[3145728]{0:T(1024)(128)(4,1)S(1)} async-done(((s8[7340032]{0:T(1024)(128)(4,1)}), s8[3145728]{0:T(1024)(128)(4,1)S(1)}, s32[]{:S(2)}) %slice-start.5) | async-done | bytes 3145752
  63.9 2.5 %multiply_reduce_fusion = (bf16[64]{0:T(256)(128)(2,1)S(1)}, f32[64,512]{1,0:T(8,128)S(1)}) fusion(f32[64,512]{1,0:T(8,128)S(1)} %fusion.8, f32[64,512]{1,0:T(8,128)S(1)} %fusion.5, bf16[64,7168]{1,0:T(8,128)(2,1)S(1)} %bitcast.117, bf16[1,512,7168]{2,1,0:T(8,128)(2,1)S(1)} %bitcast.116), kind=kOutput, calls=%fused_computation.59 | convolution fusion | flops 469991360 | bytes 8650880 | tf_op jit(solution)/shard_map/dot_general | solution.py:22
  66.4 2.3 %fusion.3 = f32[64,7168]{1,0:T(8,128)S(1)} fusion(bf16[1,7168,512]{2,1,0:T(8,128)(2,1)S(1)} %bitcast.110, f32[64,512]{1,0:T(8,128)S(1)} %fusion.5, f32[64,512]{1,0:T(8,128)S(1)} %get-tuple-element.27, f32[64,512]{1,0:T(8,128)S(1)} %fusion.8), kind=kOutput, calls=%fused_computation.4 | convolution fusion | flops 470089728 | bytes 9568256 | tf_op jit(solution)/shard_map/dot_general | solution.py:32
  68.7 2.3 %fusion.2 = bf16[64,7168]{1,0:T(8,128)(2,1)S(1)} fusion(f32[64,7168]{1,0:T(8,128)S(1)} %fusion.3, bf16[1,7168,512]{2,1,0:T(8,128)(2,1)S(1)} %bitcast.112, f32[64,512]{1,0:T(8,128)S(1)} %get-tuple-element.27, f32[64,512]{1,0:T(8,128)S(1)} %fusion.5), kind=kOutput, calls=%fused_computation.3 | convolution fusion | flops 470876160 | bytes 10354688 | tf_op jit(solution)/shard_map/dot_general | solution.py:34
  71.2 1.1 maximum_bitcast_fusion
  72.2 3.6 %all-to-all-start.1 = ((bf16[4,64,1920]{2,1,0:T(8,128)(2,1)}), bf16[4,64,1920]{2,1,0:T(8,128)(2,1)S(1)}, u32[]{:S(2)}, u32[]{:S(2)}) async-start(bf16[4,64,1920]{2,1,0:T(8,128)(2,1)} %maximum_bitcast_fusion), calls=%async_computation.1 | async-start | bytes 1966080 | tf_op jit(solution)/shard_map/all_to_all | solution.py:75
  76.0 1.8 %copy.71 = f32[128,576]{0,1:T(8,128)} copy(f32[128,576]{1,0:T(8,128)} %reduce-scatter.5.cloned.1.call-done) | data formatting | bytes 589824
  77.8 11.8 %all-to-all-done.1 = bf16[4,64,1920]{2,1,0:T(8,128)(2,1)S(1)} async-done(((bf16[4,64,1920]{2,1,0:T(8,128)(2,1)}), bf16[4,64,1920]{2,1,0:T(8,128)(2,1)S(1)}, u32[]{:S(2)}, u32[]{:S(2)}) %all-to-all-start.1) | async-done | bytes 983072 | tf_op jit(solution)/shard_map/all_to_all | solution.py:75
  89.6 0.9 reduce_sum.77
  90.5 5.7 %all-to-all-start.2 = ((bf16[8,8,1920]{2,1,0:T(8,128)(2,1)}), bf16[8,8,1920]{2,1,0:T(8,128)(2,1)S(1)}, u32[]{:S(2)}, u32[]{:S(2)}) async-start(bf16[8,8,1920]{2,1,0:T(8,128)(2,1)} %bitcast.10), calls=%async_computation.2 | async-start | bytes 491520 | tf_op jit(solution)/shard_map/all_to_all | solution.py:78
  96.2 3.3 %convolution_convert_fusion.4 = bf16[8,192,256]{2,1,0:T(8,128)(2,1)S(1)} fusion(f32[8,256,256]{2,1,0:T(8,128)S(1)} %fusion.73, bf16[256,8,64]{0,2,1:T(8,128)(2,1)S(1)} %copy-done.10, bf16[256,8,128]{0,2,1:T(8,128)(2,1)} %bitcast.133, f32[8,256,256]{1,2,0:T(8,128)} %get-tuple-element.29, f32[8,256]{1,0:T(8,128)S(1)} %get-tuple-element.28), kind=kOutput, calls=%fused_computation.30 | convolution fusion | flops 206964992 | bytes 5775360 | tf_op jit(solution)/shard_map/hqk,khd->qhd/dot_general | solution.py:142
  99.5 1.2 %copy.65 = bf16[256,1536]{1,0:T(8,128)(2,1)} copy(bf16[256,1536]{0,1:T(8,128)(2,1)S(1)} %bitcast.130) | data formatting | bytes 1572864
  100.7 1.2 %reduce-scatter.7.cloned.1.call-done = f32[144,128]{1,0:T(8,128)} async-done(((f32[576,128]{1,0:T(8,128)}), f32[144,128]{1,0:T(8,128)}) %reduce-scatter.7.cloned.1.call-update) | async-done | bytes 73744
  101.8 1.0 copy.72
  103.5 1.1 all-to-all-done.2
  105.7 1.1 convolution_convert_fusion.2
  (80 shorter events, 9.2 us)
Async XLA Ops:
  8.0 10.9 %copy-start.11 = (bf16[128,576]{0,1:T(8,128)(2,1)S(1)}, bf16[128,576]{0,1:T(8,128)(2,1)}, u32[]{:S(2)}) copy-start(bf16[128,576]{0,1:T(8,128)(2,1)} %param.20) | copy-start | bytes 442372
  8.0 21.3 %copy-start.5 = (bf16[256,1024]{1,0:T(8,128)(2,1)S(1)}, bf16[256,1024]{1,0:T(8,128)(2,1)}, u32[]{:S(2)}) copy-start(bf16[256,1024]{1,0:T(8,128)(2,1)} %param.22) | copy-start | bytes 1572868
  8.0 21.5 %copy-start.3 = (bf16[256,1536]{1,0:T(8,128)(2,1)S(1)}, bf16[256,1536]{1,0:T(8,128)(2,1)}, u32[]{:S(2)}) copy-start(bf16[256,1536]{1,0:T(8,128)(2,1)} %param.21) | copy-start | bytes 2359300
  11.4 21.3 %copy-start.13 = (s32[256]{0:T(256)S(1)}, s32[256]{0:T(256)}, u32[]{:S(2)}) copy-start(s32[256]{0:T(256)} %param.25) | copy-start | bytes 3076
  11.4 21.4 %copy-start.1 = (bf16[512,1024]{1,0:T(8,128)(2,1)S(1)}, bf16[512,1024]{1,0:T(8,128)(2,1)}, u32[]{:S(2)}) copy-start(bf16[512,1024]{1,0:T(8,128)(2,1)} %param.23) | copy-start | bytes 3145732
  11.4 20.5 %all-to-all-start = ((bf16[8,8,3584]{2,1,0:T(8,128)(2,1)}), bf16[8,8,3584]{2,1,0:T(8,128)(2,1)S(1)}, u32[]{:S(2)}, u32[]{:S(2)}) async-start(bf16[8,8,3584]{2,1,0:T(8,128)(2,1)} %fusion.12), calls=%async_computation | async-start | bytes 917504 | tf_op jit(solution)/shard_map/all_to_all | solution.py:65
  18.8 34.6 %all-gather.2.cloned.1.call-start = ((), (), s32[]{:S(2)}) async-start(), calls=%async_computation.5 | async-start | bytes 2293760 | tf_op jit(solution)/shard_map/all_gather | solution.py:66
  28.6 0.7 copy-start.7
  29.5 3.3 %copy-start.8 = (bf16[256,576]{0,1:T(8,128)(2,1)S(1)}, bf16[256,576]{0,1:T(8,128)(2,1)}, u32[]{:S(2)}) copy-start(bf16[256,576]{0,1:T(8,128)(2,1)} %copy-done.7) | copy-start | bytes 884740
  31.9 0.8 copy-start
  32.7 43.3 %reduce-scatter.5.cloned.1.call-start = ((), (), s32[]{:S(2)}) async-start(), calls=%async_computation.6 | async-start | bytes 983040 | tf_op jit(solution)/shard_map/reduce_scatter | solution.py:166
  34.9 0.8 slice-start.6
  34.9 1.1 %copy-start.4 = (bf16[256,1536]{0,1:T(8,128)(2,1)S(1)}, bf16[256,1536]{0,1:T(8,128)(2,1)}, u32[]{:S(2)}) copy-start(bf16[256,1536]{0,1:T(8,128)(2,1)} %copy.56) | copy-start | bytes 2359300
  35.6 2.6 %copy-start.6 = (bf16[256,1024]{0,1:T(8,128)(2,1)}, bf16[256,1024]{0,1:T(8,128)(2,1)S(1)}, u32[]{:S(2)}) copy-start(bf16[256,1024]{0,1:T(8,128)(2,1)S(1)} %get-tuple-element.24) | copy-start | bytes 1572868
  35.6 2.6 %copy-start.9 = (bf16[256,8,64]{0,2,1:T(8,128)(2,1)}, bf16[256,8,64]{0,2,1:T(8,128)(2,1)S(1)}, u32[]{:S(2)}) copy-start(bf16[256,8,64]{0,2,1:T(8,128)(2,1)S(1)} %broadcast_in_dim.104) | copy-start | bytes 786436
  45.4 1.9 %copy-start.15 = (f32[8,256,256]{1,2,0:T(8,128)S(1)}, f32[8,256,256]{1,2,0:T(8,128)}, u32[]{:S(2)}) copy-start(f32[8,256,256]{1,2,0:T(8,128)} %get-tuple-element.29) | copy-start | bytes 6291460
  47.3 1.2 %copy-start.2 = (bf16[512,1024]{1,0:T(8,128)(2,1)S(1)}, bf16[512,1024]{1,0:T(8,128)(2,1)}, u32[]{:S(2)}) copy-start(bf16[512,1024]{1,0:T(8,128)(2,1)} %param.24) | copy-start | bytes 3145732
  55.0 4.7 %slice-start.2 = ((s8[7340032]{0:T(1024)(128)(4,1)}), s8[4194304]{0:T(1024)(128)(4,1)S(1)}, s32[]{:S(2)}) async-start(s8[7340032]{0:T(1024)(128)(4,1)} %bitcast.111), calls=%async_computation.10 | async-start | bytes 8388608
  55.1 5.2 %slice-start.3 = ((s8[7340032]{0:T(1024)(128)(4,1)}), s8[3145728]{0:T(1024)(128)(4,1)S(1)}, s32[]{:S(2)}) async-start(s8[7340032]{0:T(1024)(128)(4,1)} %bitcast.111), calls=%async_computation.11 | async-start | bytes 6291456
  55.1 6.7 %slice-start.4 = ((s8[7340032]{0:T(1024)(128)(4,1)}), s8[4194304]{0:T(1024)(128)(4,1)S(1)}, s32[]{:S(2)}) async-start(s8[7340032]{0:T(1024)(128)(4,1)} %bitcast.115), calls=%async_computation.12 | async-start | bytes 8388608
  55.1 11.2 %slice-start = ((s8[7340032]{0:T(1024)(128)(4,1)}), s8[4194304]{0:T(1024)(128)(4,1)S(1)}, s32[]{:S(2)}) async-start(s8[7340032]{0:T(1024)(128)(4,1)} %bitcast.109), calls=%async_computation.8 | async-start | bytes 8388608
  60.3 3.6 %slice-start.5 = ((s8[7340032]{0:T(1024)(128)(4,1)}), s8[3145728]{0:T(1024)(128)(4,1)S(1)}, s32[]{:S(2)}) async-start(s8[7340032]{0:T(1024)(128)(4,1)} %bitcast.115), calls=%async_computation.13 | async-start | bytes 6291456
  60.3 6.0 %slice-start.1 = ((s8[7340032]{0:T(1024)(128)(4,1)}), s8[3145728]{0:T(1024)(128)(4,1)S(1)}, s32[]{:S(2)}) async-start(s8[7340032]{0:T(1024)(128)(4,1)} %bitcast.109), calls=%async_computation.9 | async-start | bytes 6291456
  72.2 23.9 %copy-start.10 = (bf16[256,8,64]{0,2,1:T(8,128)(2,1)S(1)}, bf16[256,8,64]{0,2,1:T(8,128)(2,1)}, u32[]{:S(2)}) copy-start(bf16[256,8,64]{0,2,1:T(8,128)(2,1)} %copy-done.9) | copy-start | bytes 786436
  72.2 17.4 %all-to-all-start.1 = ((bf16[4,64,1920]{2,1,0:T(8,128)(2,1)}), bf16[4,64,1920]{2,1,0:T(8,128)(2,1)S(1)}, u32[]{:S(2)}, u32[]{:S(2)}) async-start(bf16[4,64,1920]{2,1,0:T(8,128)(2,1)} %maximum_bitcast_fusion), calls=%async_computation.1 | async-start | bytes 1966080 | tf_op jit(solution)/shard_map/all_to_all | solution.py:75
  75.9 25.9 %reduce-scatter.7.cloned.1.call-start = ((), (), s32[]{:S(2)}) async-start(), calls=%async_computation.7 | async-start | bytes 368640
  90.5 14.2 %all-to-all-start.2 = ((bf16[8,8,1920]{2,1,0:T(8,128)(2,1)}), bf16[8,8,1920]{2,1,0:T(8,128)(2,1)S(1)}, u32[]{:S(2)}, u32[]{:S(2)}) async-start(bf16[8,8,1920]{2,1,0:T(8,128)(2,1)} %bitcast.10), calls=%async_computation.2 | async-start | bytes 491520 | tf_op jit(solution)/shard_map/all_to_all | solution.py:78
  99.5 5.5 %copy-start.12 = (s32[128,8]{0,1:T(8,128)S(1)}, s32[128,8]{0,1:T(8,128)}, u32[]{:S(2)}) copy-start(s32[128,8]{0,1:T(8,128)} %param.15) | copy-start | bytes 12292
  99.5 5.5 %copy-start.14 = (f32[128,8]{0,1:T(8,128)S(1)}, f32[128,8]{0,1:T(8,128)}, u32[]{:S(2)}) copy-start(f32[128,8]{0,1:T(8,128)} %param.16) | copy-start | bytes 12292
Sparse Core Ops, SparseCore 0:
  32.8 20.5 all-gather.1
  79.9 21.8 reduce-scatter.6
Sparse Core Ops, SparseCore 1:
  50.1 15.3 reduce-scatter.4

commit v2 on v1

--- a/solution.py
+++ b/solution.py
@@ -1,8 +1,11 @@
+import functools
 import math
 
 import jax
 import jax.numpy as jnp
 from jax import lax
+from jax.experimental import pallas as pl
+from jax.experimental.pallas import tpu as pltpu
 from jax.sharding import PartitionSpec as P
 
 TOP = 8
@@ -16,23 +19,263 @@
 CONTRACT_LAST = (((1,), (1,)), ((), ()))
 
 
-def expert_backward(rows_x, rows_dy, gate_mat, up_mat, down_mat):
-    gate_pre = jnp.dot(rows_x, gate_mat, preferred_element_type=jnp.float32)
-    up_pre = jnp.dot(rows_x, up_mat, preferred_element_type=jnp.float32)
-    back_hidden = lax.dot_general(
-        rows_dy, down_mat, CONTRACT_LAST, preferred_element_type=jnp.float32
-    )
+MESH = pl.DeviceIdType.MESH
+LANES = 128
+
+
+def greet(peers):
+    barrier = pltpu.get_barrier_semaphore()
+    for peer in peers:
+        pl.semaphore_signal(barrier, inc=1, device_id=peer, device_id_type=MESH)
+
+
+def met(peers):
+    pl.semaphore_wait(pltpu.get_barrier_semaphore(), len(peers))
+
+
+def window_peers(experts, window):
+    me = lax.axis_index("dp") * experts + lax.axis_index("expert")
+    spots = [lax.rem(me + d, window) for d in range(1, window)]
+    head = lax.axis_index("head")
+    return me, spots, [(spot // experts, lax.rem(spot, experts), head) for spot in spots]
+
+
+def dispatch_kernel(
+    experts, window, send_ref, lat_ref, got_ref, piece_ref, out_sem, in_sem, lat_out, lat_in, own
+):
+    me, spots, peers = window_peers(experts, window)
+    dp, expert, head = (lax.axis_index(name) for name in ("dp", "expert", "head"))
+    greet(peers)
+    own_rows = pltpu.make_async_copy(send_ref.at[me], got_ref.at[me], own.at[0])
+    own_lat = pltpu.make_async_copy(lat_ref, piece_ref.at[expert], own.at[1])
+    own_rows.start()
+    own_lat.start()
+    met(peers)
+    copies = []
+    for d in range(1, experts):
+        copies.append(
+            pltpu.make_async_remote_copy(
+                src_ref=lat_ref,
+                dst_ref=piece_ref.at[expert],
+                send_sem=lat_out.at[d - 1],
+                recv_sem=lat_in.at[d - 1],
+                device_id=(dp, lax.rem(expert + d, experts), head),
+                device_id_type=MESH,
+            )
+        )
+    for num, (spot, peer) in enumerate(zip(spots, peers)):
+        copies.append(
+            pltpu.make_async_remote_copy(
+                src_ref=send_ref.at[spot],
+                dst_ref=got_ref.at[me],
+                send_sem=out_sem.at[num],
+                recv_sem=in_sem.at[num],
+                device_id=peer,
+                device_id_type=MESH,
+            )
+        )
+    for copy in copies:
+        copy.start()
+    own_rows.wait()
+    own_lat.wait()
+    for copy in copies:
+        copy.wait()
+
+
+def dispatch(send, latent):
+    experts = lax.axis_size("expert")
+    window = lax.axis_size("dp") * experts
+    hbm = pl.BlockSpec(memory_space=pl.ANY)
+    return pl.pallas_call(
+        functools.partial(dispatch_kernel, experts, window),
+        out_shape=(
+            jax.ShapeDtypeStruct(send.shape, send.dtype),
+            jax.ShapeDtypeStruct((experts,) + latent.shape, latent.dtype),
+        ),
+        in_specs=[hbm, hbm],
+        out_specs=(hbm, hbm),
+        scratch_shapes=[
+            pltpu.SemaphoreType.DMA((window - 1,)),
+            pltpu.SemaphoreType.DMA((window - 1,)),
+            pltpu.SemaphoreType.DMA((experts - 1,)),
+            pltpu.SemaphoreType.DMA((experts - 1,)),
+            pltpu.SemaphoreType.DMA((2,)),
+        ],
+        compiler_params=pltpu.CompilerParams(collective_id=1, has_side_effects=True),
+        name="dispatch",
+    )(send, latent)
+
+
+def expert_kernel(
+    experts,
+    window,
+    heads,
+    got_ref,
+    wg_ref,
+    wu_ref,
+    wd_ref,
+    back_ref,
+    rows_buf,
+    wg_buf,
+    wu_buf,
+    wd_buf,
+    part_buf,
+    land_buf,
+    sum_buf,
+    back_buf,
+    load_sem,
+    part_out,
+    part_in,
+    back_out,
+    back_in,
+):
+    me, spots, peers = window_peers(experts, window)
+    dp, expert, head = (lax.axis_index(name) for name in ("dp", "expert", "head"))
+    width = got_ref.shape[3]
+    slots = window * CAP
+    half = width // 2
+    order = list(range(heads))
+    spot_of = [lax.rem(head + d, heads) for d in order]
+    head_peers = [(dp, expert, spot_of[d]) for d in order]
+    everyone = head_peers[1:] + peers
+    loads = []
+    for d in order:
+        cols = pl.ds(pl.multiple_of(spot_of[d] * width, LANES), width)
+        loads.append(
+            [
+                pltpu.make_async_copy(got_ref.at[spot_of[d]], rows_buf.at[d], load_sem.at[0, d]),
+                pltpu.make_async_copy(wg_ref.at[0, cols, :], wg_buf.at[d], load_sem.at[1, d]),
+                pltpu.make_async_copy(wu_ref.at[0, cols, :], wu_buf.at[d], load_sem.at[2, d]),
+                pltpu.make_async_copy(wd_ref.at[0, :, cols], wd_buf.at[d], load_sem.at[3, d]),
+            ]
+        )
+        for copy in loads[d]:
+            copy.start()
+    greet(everyone)
+    gate_pre = up_pre = back_hidden = None
+    for d in order:
+        loads[d][0].wait()
+        rows = rows_buf[d].astype(jnp.float32)
+        rows_x = rows[:, :CAP].reshape(slots, width).astype(jnp.bfloat16)
+        rows_dy = rows[:, CAP:].reshape(slots, width).astype(jnp.bfloat16)
+        loads[d][1].wait()
+        term = jnp.dot(rows_x, wg_buf[d], preferred_element_type=jnp.float32)
+        gate_pre = term if d == 0 else gate_pre + term
+        loads[d][2].wait()
+        term = jnp.dot(rows_x, wu_buf[d], preferred_element_type=jnp.float32)
+        up_pre = term if d == 0 else up_pre + term
+        loads[d][3].wait()
+        term = lax.dot_general(
+            rows_dy, wd_buf[d], CONTRACT_LAST, preferred_element_type=jnp.float32
+        )
+        back_hidden = term if d == 0 else back_hidden + term
     sig_val = jax.nn.sigmoid(gate_pre)
     act_val = gate_pre * sig_val
-    gate_part = jnp.sum(act_val * up_pre * back_hidden, axis=1)
+    gate_part = jnp.sum(act_val * up_pre * back_hidden, axis=1, keepdims=True)
     d_up = (back_hidden * act_val).astype(jnp.bfloat16)
     d_pre = (back_hidden * up_pre * sig_val * (1.0 + gate_pre * (1.0 - sig_val))).astype(
         jnp.bfloat16
     )
-    row_part = lax.dot_general(
-        d_pre, gate_mat, CONTRACT_LAST, preferred_element_type=jnp.float32
-    ) + lax.dot_general(d_up, up_mat, CONTRACT_LAST, preferred_element_type=jnp.float32)
-    return (row_part, gate_part)
+    gate_high = gate_part.astype(jnp.bfloat16).astype(jnp.float32)
+    lane = lax.broadcasted_iota(jnp.int32, (slots, LANES), 1)
+    gate_cols = jnp.where(lane < LANES // 2, gate_high, gate_part - gate_high)
+    met(everyone)
+    copies = []
+    for d in order[1:] + [0]:
+        part = lax.dot_general(
+            d_pre, wg_buf[d], CONTRACT_LAST, preferred_element_type=jnp.float32
+        ) + lax.dot_general(d_up, wu_buf[d], CONTRACT_LAST, preferred_element_type=jnp.float32)
+        if d == 0:
+            total, gate_total = part, gate_cols
+            continue
+        part_buf[d - 1, :, :width] = part.astype(jnp.bfloat16)
+        part_buf[d - 1, :, width:] = gate_cols.astype(jnp.bfloat16)
+        copies.append(
+            pltpu.make_async_remote_copy(
+                src_ref=part_buf.at[d - 1],
+                dst_ref=land_buf.at[d - 1],
+                send_sem=part_out.at[d - 1],
+                recv_sem=part_in.at[d - 1],
+                device_id=head_peers[d],
+                device_id_type=MESH,
+            )
+        )
+        copies[-1].start()
+    for d in order[1:]:
+        copies[d - 1].wait()
+        total = total + land_buf[d - 1, :, :width].astype(jnp.float32)
+        gate_total = gate_total + land_buf[d - 1, :, width:].astype(jnp.float32)
+    gate_sum = gate_total[:, :1] + gate_total[:, LANES // 2 : LANES // 2 + 1]
+    gate_cols = jnp.broadcast_to(gate_sum, (slots, LANES)).reshape(window, CAP, LANES)
+    total = total.reshape(window, CAP, width)
+    packed = jnp.concatenate(
+        [
+            jnp.concatenate([total[:, :, :half], gate_cols], axis=2),
+            jnp.concatenate([total[:, :, half:], gate_cols], axis=2),
+        ],
+        axis=1,
+    ).astype(jnp.bfloat16)
+    sum_buf[...] = packed
+    copies = []
+    for num, (spot, peer) in enumerate(zip(spots, peers)):
+        copies.append(
+            pltpu.make_async_remote_copy(
+                src_ref=sum_buf.at[spot],
+                dst_ref=back_buf.at[me],
+                send_sem=back_out.at[num],
+                recv_sem=back_in.at[num],
+                device_id=peer,
+                device_id_type=MESH,
+            )
+        )
+        copies[-1].start()
+    own = pltpu.make_async_copy(sum_buf.at[me], back_buf.at[me], load_sem.at[0, 0])
+    own.start()
+    own.wait()
+    for copy in copies:
+        copy.wait()
+    back_ref[...] = back_buf[...]
+
+
+def expert_backward(got, w_gate, w_up, w_down):
+    experts = lax.axis_size("expert")
+    window = lax.axis_size("dp") * experts
+    heads, _, tile, width = got.shape
+    hidden = w_gate.shape[2]
+    slots = window * CAP
+    hbm = pl.BlockSpec(memory_space=pl.ANY)
+    back = (window, tile, width // 2 + LANES)
+    dma = pltpu.SemaphoreType.DMA
+    return pl.pallas_call(
+        functools.partial(expert_kernel, experts, window, heads),
+        out_shape=jax.ShapeDtypeStruct(back, jnp.bfloat16),
+        in_specs=[hbm] * 4,
+        out_specs=pl.BlockSpec(memory_space=pltpu.VMEM),
+        scratch_shapes=[
+            pltpu.VMEM((heads, window, tile, width), jnp.bfloat16),
+            pltpu.VMEM((heads, width, hidden), jnp.bfloat16),
+            pltpu.VMEM((heads, width, hidden), jnp.bfloat16),
+            pltpu.VMEM((heads, hidden, width), jnp.bfloat16),
+            pltpu.VMEM((heads - 1, slots, width + LANES), jnp.bfloat16),
+            pltpu.VMEM((heads - 1, slots, width + LANES), jnp.bfloat16),
+            pltpu.VMEM(back, jnp.bfloat16),
+            pltpu.VMEM(back, jnp.bfloat16),
+            dma((4, heads)),
+            dma((heads - 1,)),
+            dma((heads - 1,)),
+            dma((window - 1,)),
+            dma((window - 1,)),
+        ],
+        compiler_params=pltpu.CompilerParams(
+            collective_id=2, has_side_effects=True, vmem_limit_bytes=56 * 1024 * 1024
+        ),
+        cost_estimate=pl.CostEstimate(
+            flops=10 * slots * hidden * width * heads,
+            bytes_accessed=6 * hidden * width * heads,
+            transcendentals=slots * hidden,
+        ),
+        name="experts",
+    )(got, w_gate, w_up, w_down)
 
 
 def routing(expert_ids, gate_weights, window_size):
@@ -50,54 +293,47 @@
     return (hits, combine, names)
 
 
-def expert_half(hidden_in, grad_out, expert_ids, gate_weights, w_gate, w_up, w_down):
-    window_size = lax.axis_size("dp") * lax.axis_size("expert")
-    head_count = lax.axis_size("head")
+def expert_send(hidden_in, grad_out, hits):
     tok_local, width = hidden_in.shape
-    slots = window_size * CAP
-    hits, combine, names = routing(expert_ids, gate_weights, window_size)
+    window_size = hits.shape[1] // CAP
     pick = hits.astype(jnp.bfloat16)
     rows = jnp.concatenate([hidden_in, grad_out], axis=1)
     send = lax.dot_general(
         pick, rows, (((0,), (0,)), ((), ())), preferred_element_type=jnp.float32
     ).astype(jnp.bfloat16)
     send = send.reshape(window_size, CAP, 2 * width)
-    got = lax.all_to_all(send, ("dp", "expert"), split_axis=0, concat_axis=0, tiled=True)
-    got = lax.all_gather(got.reshape(slots, 2 * width), "head", axis=0, tiled=False)
-    flat_x = got[:, :, :width].transpose(1, 0, 2).reshape(slots, head_count * width)
-    flat_dy = got[:, :, width:].transpose(1, 0, 2).reshape(slots, head_count * width)
-    row_part, gate_part = expert_backward(flat_x, flat_dy, w_gate[0], w_up[0], w_down[0])
-    parts = row_part.astype(jnp.bfloat16).reshape(slots, head_count, width)
-    gate_cols = jnp.broadcast_to(
-        gate_part.astype(jnp.bfloat16)[:, None, None], (slots, head_count, 128)
-    )
-    parts = jnp.concatenate([parts, gate_cols], axis=2).transpose(1, 0, 2)
-    parts = lax.all_to_all(parts, "head", split_axis=0, concat_axis=0, tiled=True)
-    summed = jnp.sum(parts.astype(jnp.float32), axis=0).astype(jnp.bfloat16)
-    summed = summed.reshape(window_size, CAP, width + 128)
-    back = lax.all_to_all(summed, ("dp", "expert"), split_axis=0, concat_axis=0, tiled=True)
-    back = back.reshape(slots, width + 128)
+    return jnp.concatenate([send[:, :, :width], send[:, :, width:]], axis=1)
+
+
+def expert_half(got, hits, combine, names, w_gate, w_up, w_down):
+    tok_local, _, window_size = names.shape
+    slots = window_size * CAP
+    got = lax.all_gather(got, "head", axis=0, tiled=False)
+    back = expert_backward(got, w_gate, w_up, w_down)
+    half = back.shape[2] - LANES
+    flat_back = jnp.concatenate([back[:, :CAP, :half], back[:, CAP:, :half]], axis=2)
+    flat_back = flat_back.reshape(slots, 2 * half)
+    flat_gate = back[:, :CAP, half].reshape(slots)
     high = combine.astype(jnp.bfloat16)
     rest = combine - high.astype(jnp.float32)
     low = rest.astype(jnp.bfloat16)
-    flat_back = back[:, :width]
     d_hidden = jnp.dot(
         jnp.concatenate([high, low], axis=1),
         jnp.concatenate([flat_back, flat_back], axis=0),
         preferred_element_type=jnp.float32,
     ).astype(jnp.bfloat16)
-    gate_of = jnp.where(hits, back[:, width].astype(jnp.float32)[None, :], 0.0)
+    gate_of = jnp.where(hits, flat_gate.astype(jnp.float32)[None, :], 0.0)
     gate_of = jnp.sum(gate_of.reshape(tok_local, window_size, CAP), axis=2)
     d_gates = jnp.sum(jnp.where(names, gate_of[:, None, :], 0.0), axis=2).astype(jnp.bfloat16)
     return (d_hidden, d_gates)
 
 
-def attention_half(latent_kv, query, d_attn, w_uk, w_uv, doc_ids):
+def attention_half(latent_kv, piece, query, d_attn, w_uk, w_uv, doc_ids):
     seq_len = query.shape[0]
     heads_here = w_uk.shape[1] // NOPE
     score_scale = 1.0 / math.sqrt(NOPE + ROPE)
     w_both = jnp.concatenate([w_uk, w_uv], axis=1)
-    piece = lax.all_gather(latent_kv, "expert", axis=0, tiled=True)
+    piece = piece.reshape(seq_len, piece.shape[2])
     lifted = jnp.dot(piece[:, :LAT], w_both, preferred_element_type=jnp.float32).astype(
         jnp.bfloat16
     )
@@ -185,10 +421,12 @@
     w_uv,
     doc_ids,
 ):
-    d_query, d_latent_kv = attention_half(latent_kv, query, d_attn, w_uk, w_uv, doc_ids)
-    d_hidden, d_gates = expert_half(
-        hidden_in, grad_out, expert_ids, gate_weights, w_gate, w_up, w_down
-    )
+    window_size = lax.axis_size("dp") * lax.axis_size("expert")
+    hits, combine, names = routing(expert_ids, gate_weights, window_size)
+    send = expert_send(hidden_in, grad_out, hits)
+    got, piece = dispatch(send, latent_kv)
+    d_query, d_latent_kv = attention_half(latent_kv, piece, query, d_attn, w_uk, w_uv, doc_ids)
+    d_hidden, d_gates = expert_half(got, hits, combine, names, w_gate, w_up, w_down)
     return (d_hidden, d_gates, d_query, d_latent_kv)
 
 

time: 115 us -> 155 us (1.35)
  Pallas kernels: 0 us -> 44.9 us
  waiting for transfers between devices: 18.8 us -> 55.6 us
  starting transfers between devices: 16.8 us -> 0.3 us
  matrix products: 32 us -> 20.9 us
  blocking collectives: 9.75 us -> 0 us
  local copies, waits for them, and re-layouts: 15.4 us -> 13 us
  between operations: 15.9 us -> 14 us
    pallas_call x0 -> x2, Pallas kernels: none -> 44.9 us  [the longest x1 29 us: expert_backward(): pl.pallas_call(functools.partial(expert_kernel, experts, window, heads),...]
    all_gather x1, waiting for transfers between devices: 3.44 us -> 21 us  [expert_half(): got = lax.all_gather(got, 'head', axis=0, tiled=False)]
    reduce_scatter x1, waiting for transfers between devices: 0.03 us -> 17.5 us  [attention_half(): lax.psum_scatter(jnp.concatenate([lat_term, rope_term], axis=1), 'expert'...]
    all_to_all x3 -> x0, starting transfers between devices: 16.7 us -> none  [the longest x1 7.38 us: expert_half(): lax.all_to_all(send, ('dp', 'expert'), split_axis=0, concat_axis=0, tiled...]
    unnamed x4, waiting for transfers between devices: 1.22 us -> 17 us
    all_to_all x3 -> x0, waiting for transfers between devices: 14.1 us -> none  [the longest x1 11.8 us: expert_half(): lax.all_to_all(parts, 'head', split_axis=0, concat_axis=0, tiled=True)]
    dot_general x6 -> x1, matrix products: 15.4 us -> 1.51 us  [expert_send(): lax.dot_general(pick, rows, (((0,), (0,)), ((), ())), preferred_element_t...]
    all_gather x1 -> x0, blocking collectives: 9.75 us -> none  [attention_half(): piece = lax.all_gather(latent_kv, 'expert', axis=0, tiled=True)]
  transfers between devices with their start and end apart: 6 -> 3, of which waited for: 5 -> 3; matrix products, arithmetic and copies ran while one was open for 36% -> 4% of each run, Pallas kernels for 0% -> 0%
where the time goes in v2:
time: 155 us; the launch traced here: 154 us
  waiting for transfers between devices  55.6 us (36%)
  Pallas kernels  44.9 us (29%)
  matrix products  20.9 us (13%)
  between operations  14 us (9%)
  local copies, waits for them, and re-layouts  13 us (8%)
  other arithmetic  5.14 us (3%)
    pallas_call x1, Pallas kernels, expert_backward(): pl.pallas_call(functools.partial(expert_kernel, experts, window, heads),...  29 us
    all_gather x1, waiting for transfers between devices, expert_half(): got = lax.all_gather(got, 'head', axis=0, tiled=False)  21 us
    reduce_scatter x1, waiting for transfers between devices, attention_half(): lax.psum_scatter(jnp.concatenate([lat_term, rope_term], axis=1), 'expert'...  17.5 us
    unnamed x4, waiting for transfers between devices  17 us
    pallas_call x1, Pallas kernels, dispatch(): pl.pallas_call(functools.partial(dispatch_kernel, experts, window), out_s...  15.8 us
    unnamed x28, local copies, waits for them, and re-layouts  6.71 us
    dot_general x1, matrix products, attention_half(): jnp.einsum('hqk,qhd->khd', dscore, query_blk, preferred_element_type=jnp....  3.93 us
    sub x1, matrix products, attention_half(): expd = jnp.exp(scores - top_score)  3.69 us
  transfers between devices with their start and end apart: 3, of which 3 were waited for; matrix products, arithmetic and copies ran while one was open for 4% of the time, Pallas kernels for 0%

profile of v2, /device:TPU:0, one launch (start us, length us, event | category | flops | bytes accessed | tf_op | source)
XLA Modules:
  0.0 153.8 jit_solution(12954304289425860523)
XLA Ops:
  7.3 0.7 fusion.38
  8.2 1.5 fusion.2
  9.8 0.8 copy.47.lat_ref
  10.6 1.2 copy.67
  11.9 0.8 pad_maximum_fusion.4.send_ref
  12.7 15.8 %dispatch.1 = (bf16[8,16,1792]{2,1,0:T(8,128)(2,1)}, bf16[2,128,576]{2,1,0:T(8,128)(2,1)}) custom-call(bf16[8,16,1792]{2,1,0:T(8,128)(2,1)} %pad_maximum_fusion.4.send_ref, bf16[128,576]{1,0:T(8,128)(2,1)} %copy.47.lat_ref), custom_call_target="tpu_custom_call" | custom-call | tf_op jit(solution)/shard_map/dispatch/pallas_call | solution.py:89
  28.5 0.8 slice.48
  29.4 1.7 %convolution_convert_fusion.1 = bf16[256,2048]{1,0:T(8,128)(2,1)S(1)} fusion(bf16[512,1024]{1,0:T(8,128)(2,1)S(1)} %copy-done.1, bf16[512,1024]{1,0:T(8,128)(2,1)S(1)} %copy-done, bf16[256,576]{1,0:T(8,128)(2,1)} %bitcast.92), kind=kOutput, calls=%fused_computation.4 | convolution fusion | flops 541589504 | bytes 3407872 | tf_op jit(solution)/shard_map/dot_general | solution.py:337
  31.2 1.0 copy.64
  32.4 1.2 copy.50
  33.9 0.7 broadcast_in_dim.97
  34.7 3.7 %fusion.61 = (f32[8,256]{1,0:T(8,128)S(1)}, f32[8,256,256]{1,2,0:T(8,128)}) fusion(pred[256,256]{0,1:T(8,128)(4,1)S(1)} %fusion.28, bf16[256,8,192]{0,2,1:T(8,128)(2,1)} %bitcast.84, bf16[256,8,64]{0,2,1:T(8,128)(2,1)} %broadcast_in_dim.97, bf16[256,8,128]{0,2,1:T(8,128)(2,1)} %bitcast.88), kind=kOutput, calls=%fused_computation.89 | convolution fusion | flops 204996864 | bytes 3743744 | tf_op jit(solution)/shard_map/sub | solution.py:369
  38.4 3.9 %fusion.10 = bf16[256,8,192]{0,2,1:T(8,128)(2,1)} fusion(bf16[256,8,192]{0,2,1:T(8,128)(2,1)S(1)} %bitcast.85, f32[8,256,256]{2,1,0:T(8,128)S(1)} %fusion.21, f32[8,256,256]{1,2,0:T(8,128)} %get-tuple-element.29, f32[8,256]{1,0:T(8,128)S(1)} %get-tuple-element.28), kind=kOutput, calls=%fused_computation.20 | convolution fusion | flops 205392128 | bytes 5775360 | tf_op jit(solution)/shard_map/hqk,qhd->khd/dot_general | solution.py:382
  42.3 1.0 convert_reduce_fusion
  43.3 1.1 slice.50
  44.4 2.9 %convolution_convert_fusion.5 = bf16[8,256,128]{1,2,0:T(8,128)(2,1)} fusion(bf16[256,8,128]{0,2,1:T(8,128)(2,1)S(1)} %bitcast.80, f32[8,256,256]{1,2,0:T(8,128)} %get-tuple-element.29, f32[8,256]{1,0:T(8,128)S(1)} %get-tuple-element.28), kind=kOutput, calls=%fused_computation.19 | convolution fusion | flops 135528448 | bytes 3153920 | tf_op jit(solution)/shard_map/hqk,qhd->khd/dot_general | solution.py:385
  47.4 1.8 %fusion.62 = f32[256,512]{1,0:T(8,128)S(1)} fusion(bf16[256,1024]{0,1:T(8,128)(2,1)S(1)} %bitcast.81, bf16[512,1024]{1,0:T(8,128)(2,1)} %param.23), kind=kOutput, calls=%fused_computation.90 | convolution fusion | flops 268435456 | bytes 2097152 | tf_op jit(solution)/shard_map/dot_general | solution.py:393
  49.7 0.9 pad_maximum_fusion.1
  50.7 17.5 %reduce-scatter.5.cloned.1.call-done = f32[128,576]{1,0:T(8,128)} async-done(((f32[256,576]{1,0:T(8,128)}), f32[128,576]{1,0:T(8,128)}) %reduce-scatter.5.cloned.1.call-update) | async-done | bytes 294928 | tf_op jit(solution)/shard_map/reduce_scatter | solution.py:402
  68.2 1.8 %copy.65 = f32[128,576]{0,1:T(8,128)} copy(f32[128,576]{1,0:T(8,128)} %reduce-scatter.5.cloned.1.call-done) | data formatting | bytes 589824
  70.3 0.5 all-gather.3.cloned.1.call-update
  70.8 3.2 %convolution_convert_fusion.4 = bf16[8,192,256]{2,1,0:T(8,128)(2,1)S(1)} fusion(f32[8,256,256]{2,1,0:T(8,128)S(1)} %fusion.21, bf16[256,8,64]{0,2,1:T(8,128)(2,1)S(1)} %copy-done.6, bf16[256,8,128]{0,2,1:T(8,128)(2,1)} %bitcast.89, f32[8,256,256]{1,2,0:T(8,128)} %get-tuple-element.29, f32[8,256]{1,0:T(8,128)S(1)} %get-tuple-element.28), kind=kOutput, calls=%fused_computation.18 | convolution fusion | flops 206964992 | bytes 5775360 | tf_op jit(solution)/shard_map/hqk,khd->qhd/dot_general | solution.py:378
  74.1 1.2 copy.59
  75.2 16.5 %reduce-scatter.7.cloned.1.call-done = f32[144,128]{1,0:T(8,128)} async-done(((f32[576,128]{1,0:T(8,128)}), f32[144,128]{1,0:T(8,128)}) %reduce-scatter.7.cloned.1.call-update) | async-done | bytes 73744
  91.7 1.0 copy.66
  92.7 0.7 copy.60
  93.4 21.0 %all-gather.3.cloned.1.call-done = bf16[32,16,1792]{2,1,0:T(8,128)(2,1)} async-done(((bf16[8,16,1792]{2,1,0:T(8,128)(2,1)}), bf16[32,16,1792]{2,1,0:T(8,128)(2,1)}) %all-gather.3.cloned.1.call-update) | async-done | bytes 1835024 | tf_op jit(solution)/shard_map/all_gather | solution.py:311
  114.5 29.0 %experts.1 = bf16[8,16,1024]{2,1,0:T(8,128)(2,1)} custom-call(bf16[4,8,16,1792]{3,2,1,0:T(8,128)(2,1)} %bitcast.82, bf16[1,7168,512]{2,1,0:T(8,128)(2,1)} %wg_ref.1, bf16[1,7168,512]{2,1,0:T(8,128)(2,1)} %wu_ref.1, bf16[1,512,7168]{2,1,0:T(8,128)(2,1)} %wd_ref.1), custom_call_target="tpu_custom_call" | custom-call | flops 2348810240 | bytes 22020096 | tf_op jit(solution)/shard_map/experts/pallas_call | solution.py:249
  143.5 1.0 fusion.60
  144.5 0.8 convert_reduce_fusion.1
  145.4 0.6 select_reduce_fusion
  146.2 1.1 convolution_convert_fusion.2
  (42 shorter events, 2.2 us)
Async XLA Ops:
  7.2 2.6 %copy-start.7 = (bf16[128,576]{0,1:T(8,128)(2,1)S(1)}, bf16[128,576]{0,1:T(8,128)(2,1)}, u32[]{:S(2)}) copy-start(bf16[128,576]{0,1:T(8,128)(2,1)} %param.20) | copy-start | bytes 442372
  7.2 61.0 %reduce-scatter.5.cloned.1.call-start = ((), (), s32[]{:S(2)}) async-start(), calls=%async_computation.2 | async-start | bytes 983040 | tf_op jit(solution)/shard_map/reduce_scatter | solution.py:402
  9.7 19.6 %copy-start = (bf16[512,1024]{1,0:T(8,128)(2,1)S(1)}, bf16[512,1024]{1,0:T(8,128)(2,1)}, u32[]{:S(2)}) copy-start(bf16[512,1024]{1,0:T(8,128)(2,1)} %param.23) | copy-start | bytes 3145732
  9.8 19.6 %copy-start.1 = (bf16[512,1024]{1,0:T(8,128)(2,1)S(1)}, bf16[512,1024]{1,0:T(8,128)(2,1)}, u32[]{:S(2)}) copy-start(bf16[512,1024]{1,0:T(8,128)(2,1)} %param.24) | copy-start | bytes 3145732
  31.0 1.2 copy-start.9
  31.0 1.3 copy-start.3
  34.7 3.7 %copy-start.4 = (bf16[256,1536]{0,1:T(8,128)(2,1)S(1)}, bf16[256,1536]{0,1:T(8,128)(2,1)}, u32[]{:S(2)}) copy-start(bf16[256,1536]{0,1:T(8,128)(2,1)} %copy.50) | copy-start | bytes 2359300
  47.3 1.9 %copy-start.2 = (bf16[512,1024]{1,0:T(8,128)(2,1)S(1)}, bf16[512,1024]{1,0:T(8,128)(2,1)}, u32[]{:S(2)}) copy-start(bf16[512,1024]{1,0:T(8,128)(2,1)} %param.24) | copy-start | bytes 3145732
  47.4 1.9 %copy-start.5 = (bf16[8,256,128]{1,2,0:T(8,128)(2,1)S(1)}, bf16[8,256,128]{1,2,0:T(8,128)(2,1)}, u32[]{:S(2)}) copy-start(bf16[8,256,128]{1,2,0:T(8,128)(2,1)} %convolution_convert_fusion.5) | copy-start | bytes 1572868
  49.7 21.1 %copy-start.6 = (bf16[256,8,64]{0,2,1:T(8,128)(2,1)S(1)}, bf16[256,8,64]{0,2,1:T(8,128)(2,1)}, u32[]{:S(2)}) copy-start(bf16[256,8,64]{0,2,1:T(8,128)(2,1)} %broadcast_in_dim.97) | copy-start | bytes 786436
  50.6 41.1 %reduce-scatter.7.cloned.1.call-start = ((), (), s32[]{:S(2)}) async-start(), calls=%async_computation.4 | async-start | bytes 368640
  70.1 44.4 %all-gather.3.cloned.1.call-start = ((), (), s32[]{:S(2)}) async-start(), calls=%async_computation.3 | async-start | bytes 2293760 | tf_op jit(solution)/shard_map/all_gather | solution.py:311
  114.4 30.9 %copy-start.8 = (s32[128,8]{0,1:T(8,128)S(1)}, s32[128,8]{0,1:T(8,128)}, u32[]{:S(2)}) copy-start(s32[128,8]{0,1:T(8,128)} %param.15) | copy-start | bytes 12292
  114.4 30.9 %copy-start.10 = (f32[128,8]{0,1:T(8,128)S(1)}, f32[128,8]{0,1:T(8,128)}, u32[]{:S(2)}) copy-start(f32[128,8]{0,1:T(8,128)} %param.16) | copy-start | bytes 12292
Sparse Core Ops, SparseCore 0:
  50.8 17.4 reduce-scatter.4
  71.4 20.2 reduce-scatter.6
  93.3 21.1 all-gather.2

commit v3 on v2

--- a/solution.py
+++ b/solution.py
@@ -305,11 +305,9 @@
     return jnp.concatenate([send[:, :, :width], send[:, :, width:]], axis=1)
 
 
-def expert_half(got, hits, combine, names, w_gate, w_up, w_down):
+def expert_half(back, hits, combine, names):
     tok_local, _, window_size = names.shape
     slots = window_size * CAP
-    got = lax.all_gather(got, "head", axis=0, tiled=False)
-    back = expert_backward(got, w_gate, w_up, w_down)
     half = back.shape[2] - LANES
     flat_back = jnp.concatenate([back[:, :CAP, :half], back[:, CAP:, :half]], axis=2)
     flat_back = flat_back.reshape(slots, 2 * half)
@@ -399,11 +397,10 @@
         preferred_element_type=jnp.float32,
     )
     rope_term = jnp.sum(dkey_low[:, :, NOPE:].astype(jnp.float32), axis=1)
-    own_rows = lax.psum_scatter(
-        jnp.concatenate([lat_term, rope_term], axis=1), "expert", scatter_dimension=0, tiled=True
-    )
-    d_latent = lax.psum_scatter(own_rows, "head", scatter_dimension=1, tiled=True)
-    return (d_query, d_latent.astype(jnp.bfloat16))
+    cols = latent_kv.shape[1] // lax.axis_size("head")
+    terms = jnp.concatenate([lat_term, rope_term], axis=1)
+    terms = terms.reshape(lax.axis_size("expert"), latent_kv.shape[0], lax.axis_size("head"), cols)
+    return (d_query, terms.transpose(0, 2, 1, 3).reshape(-1, cols))
 
 
 def body(
@@ -425,8 +422,15 @@
     hits, combine, names = routing(expert_ids, gate_weights, window_size)
     send = expert_send(hidden_in, grad_out, hits)
     got, piece = dispatch(send, latent_kv)
-    d_query, d_latent_kv = attention_half(latent_kv, piece, query, d_attn, w_uk, w_uv, doc_ids)
-    d_hidden, d_gates = expert_half(got, hits, combine, names, w_gate, w_up, w_down)
+    got = lax.all_gather(got, "head", axis=0, tiled=False)
+    d_query, terms = attention_half(latent_kv, piece, query, d_attn, w_uk, w_uv, doc_ids)
+    got, terms, d_query = lax.optimization_barrier((got, terms, d_query))
+    d_latent_kv = lax.psum_scatter(
+        terms, ("expert", "head"), scatter_dimension=0, tiled=True
+    ).astype(jnp.bfloat16)
+    back = expert_backward(got, w_gate, w_up, w_down)
+    back, d_latent_kv = lax.optimization_barrier((back, d_latent_kv))
+    d_hidden, d_gates = expert_half(back, hits, combine, names)
     return (d_hidden, d_gates, d_query, d_latent_kv)
 
 

time: 155 us -> 101 us (0.65)
  waiting for transfers between devices: 55.6 us -> 7.12 us
  local copies, waits for them, and re-layouts: 13 us -> 9.59 us
  matrix products: 20.9 us -> 18.9 us
    all_gather x1, waiting for transfers between devices: 21 us -> 0.02 us  [body(): got = lax.all_gather(got, 'head', axis=0, tiled=False)]
    unnamed x4 -> x2, waiting for transfers between devices: 17 us -> 0.03 us
    reduce_scatter x1, waiting for transfers between devices: 17.5 us -> 7.06 us  [body(): lax.psum_scatter(terms, ('expert', 'head'), scatter_dimension=0, tiled=True)]
    unnamed x28 -> x29, local copies, waits for them, and re-layouts: 6.71 us -> 3.1 us
    dot_general x1, matrix products: 2.88 us -> 0.5 us  [attention_half(): jnp.einsum('hqk,qhd->khd', prob_low, dout_blk, preferred_element_type=jnp...]
  transfers between devices with their start and end apart: 3 -> 2, of which waited for: 3 -> 1; matrix products, arithmetic and copies ran while one was open for 4% -> 24% of each run, Pallas kernels for 0% -> 29%
where the time goes in v3:
time: 101 us; the launch traced here: 100 us
  Pallas kernels  44.4 us (44%)
  matrix products  18.9 us (19%)
  between operations  14.3 us (14%)
  local copies, waits for them, and re-layouts  9.59 us (9%)
  waiting for transfers between devices  7.12 us (7%)
  other arithmetic  5.85 us (6%)
    pallas_call x1, Pallas kernels, expert_backward(): pl.pallas_call(functools.partial(expert_kernel, experts, window, heads),...  28.6 us
    pallas_call x1, Pallas kernels, dispatch(): pl.pallas_call(functools.partial(dispatch_kernel, experts, window), out_s...  15.8 us
    reduce_scatter x1, waiting for transfers between devices, body(): lax.psum_scatter(terms, ('expert', 'head'), scatter_dimension=0, tiled=True)  7.06 us
    dot_general x1, matrix products, attention_half(): jnp.einsum('hqk,qhd->khd', dscore, query_blk, preferred_element_type=jnp....  4.44 us
    sub x1, matrix products, attention_half(): expd = jnp.exp(scores - top_score)  3.38 us
    dot_general x1, matrix products, attention_half(): jnp.einsum('hqk,khd->qhd', dscore, all_keys, preferred_element_type=jnp.f...  3.25 us
    unnamed x29, local copies, waits for them, and re-layouts  3.1 us
  transfers between devices with their start and end apart: 2, of which 1 were waited for; matrix products, arithmetic and copies ran while one was open for 24% of the time, Pallas kernels for 29%

profile of v3, /device:TPU:0, one launch (start us, length us, event | category | flops | bytes accessed | tf_op | source)
XLA Modules:
  0.0 100.3 jit_solution(1378643265446168904)
XLA Ops:
  7.2 0.7 fusion.38
  8.3 1.7 %fusion.2 = bf16[8,8,3584]{2,1,0:T(8,128)(2,1)S(1)} fusion(bf16[128,1792]{1,0:T(8,128)(2,1)} %param.14, bf16[128,1792]{1,0:T(8,128)(2,1)} %param.13, s32[64]{0:T(128)S(1)} %eq.62, s32[128,8]{0,1:T(8,128)S(1)} %fusion.11), kind=kOutput, calls=%fused_computation.3 | convolution fusion | flops 60792832 | bytes 1380608 | tf_op jit(solution)/shard_map/dot_general | solution.py:301
  10.0 0.8 copy.61.lat_ref
  10.8 0.8 pad_maximum_fusion.4.send_ref
  11.6 15.8 %dispatch.1 = (bf16[8,16,1792]{2,1,0:T(8,128)(2,1)}, bf16[2,128,576]{2,1,0:T(8,128)(2,1)}) custom-call(bf16[8,16,1792]{2,1,0:T(8,128)(2,1)} %pad_maximum_fusion.4.send_ref, bf16[128,576]{1,0:T(8,128)(2,1)} %copy.61.lat_ref), custom_call_target="tpu_custom_call" | custom-call | tf_op jit(solution)/shard_map/dispatch/pallas_call | solution.py:89
  27.5 0.8 slice.48
  28.3 1.7 %convolution_convert_fusion.1 = bf16[256,2048]{1,0:T(8,128)(2,1)S(1)} fusion(bf16[512,1024]{1,0:T(8,128)(2,1)S(1)} %copy-done.1, bf16[512,1024]{1,0:T(8,128)(2,1)S(1)} %copy-done, bf16[256,576]{1,0:T(8,128)(2,1)} %bitcast.94), kind=kOutput, calls=%fused_computation.4 | convolution fusion | flops 541589504 | bytes 3407872 | tf_op jit(solution)/shard_map/dot_general | solution.py:335
  30.1 1.0 %copy.79 = bf16[256,1024]{0,1:T(8,128)(2,1)} copy(bf16[256,1024]{1,0:T(8,128)(2,1)S(1)} %get-tuple-element.36) | data formatting | bytes 1048576 | tf_op jit(solution)/shard_map/reshape | solution.py:339
  31.3 0.3 copy.64
  31.6 0.2 copy.80
  31.9 3.4 %fusion.61 = (f32[8,256]{1,0:T(8,128)S(1)}, f32[8,256,256]{1,2,0:T(8,128)}) fusion(pred[256,256]{0,1:T(8,128)(4,1)S(1)} %fusion.28, bf16[256,8,192]{0,2,1:T(8,128)(2,1)S(1)} %bitcast.88, bf16[256,8,64]{0,2,1:T(8,128)(2,1)S(1)} %broadcast_in_dim.96, bf16[256,8,128]{0,2,1:T(8,128)(2,1)} %bitcast.91), kind=kOutput, calls=%fused_computation.89 | convolution fusion | flops 204996864 | bytes 3743744 | tf_op jit(solution)/shard_map/sub | solution.py:367
  35.3 0.4 fusion.21
  35.7 4.4 %fusion.10 = bf16[256,8,192]{0,2,1:T(8,128)(2,1)} fusion(bf16[256,8,192]{0,2,1:T(8,128)(2,1)} %bitcast.89, f32[8,256,256]{2,1,0:T(8,128)S(1)} %fusion.21, f32[8,256,256]{1,2,0:T(8,128)} %get-tuple-element.43, f32[8,256]{1,0:T(8,128)S(1)} %get-tuple-element.42), kind=kOutput, calls=%fused_computation.20 | convolution fusion | flops 205392128 | bytes 5775360 | tf_op jit(solution)/shard_map/hqk,qhd->khd/dot_general | solution.py:380
  40.2 1.1 %slice.50 = bf16[256,8,128]{0,2,1:T(8,128)(2,1)S(1)} slice(bf16[256,8,192]{0,2,1:T(8,128)(2,1)} %fusion.10), slice={[0:256], [0:8], [0:128]} | slice | bytes 1048576 | tf_op jit(solution)/shard_map/slice | solution.py:390
  41.3 1.0 convert_reduce_fusion
  42.4 1.9 %fusion.62 = f32[256,512]{1,0:T(8,128)S(1)} fusion(bf16[256,1024]{0,1:T(8,128)(2,1)S(1)} %bitcast.85, bf16[512,1024]{1,0:T(8,128)(2,1)} %param.23), kind=kOutput, calls=%fused_computation.90 | convolution fusion | flops 268435456 | bytes 2097152 | tf_op jit(solution)/shard_map/dot_general | solution.py:391
  44.3 0.5 convolution_convert_fusion.5
  44.8 0.7 copy-done.2
  45.5 0.5 convolution_add_fusion
  46.1 0.2 copy.72
  46.3 0.3 reshape.126
  46.6 0.4 copy.73
  47.0 1.1 %reshape.127 = f32[1024,144]{0,1:T(8,128)} reshape(f32[2,4,128,144]{2,1,0,3:T(4,128)S(1)} %copy.73) | data formatting | bytes 1179648 | tf_op jit(solution)/shard_map/reshape | solution.py:403
  48.1 3.3 %convolution_convert_fusion.3 = bf16[8,192,256]{2,1,0:T(8,128)(2,1)S(1)} fusion(f32[8,256,256]{2,1,0:T(8,128)S(1)} %fusion.21, bf16[256,8,64]{0,2,1:T(8,128)(2,1)S(1)} %copy-done.7, bf16[256,8,128]{0,2,1:T(8,128)(2,1)} %bitcast.92, f32[8,256,256]{1,2,0:T(8,128)} %get-tuple-element.43, f32[8,256]{1,0:T(8,128)S(1)} %get-tuple-element.42), kind=kOutput, calls=%fused_computation.17 | convolution fusion | flops 206964992 | bytes 5775360 | tf_op jit(solution)/shard_map/hqk,khd->qhd/dot_general | solution.py:376
  51.4 1.2 %copy.75 = bf16[256,1536]{1,0:T(8,128)(2,1)} copy(bf16[256,1536]{0,1:T(8,128)(2,1)S(1)} %bitcast.87) | data formatting | bytes 1572864
  52.5 28.6 %experts.1 = bf16[8,16,1024]{2,1,0:T(8,128)(2,1)} custom-call(bf16[4,8,16,1792]{3,2,1,0:T(8,128)(2,1)} %bitcast.86, bf16[1,7168,512]{2,1,0:T(8,128)(2,1)} %wg_ref.1, bf16[1,7168,512]{2,1,0:T(8,128)(2,1)} %wu_ref.1, bf16[1,512,7168]{2,1,0:T(8,128)(2,1)} %wd_ref.1), custom_call_target="tpu_custom_call" | custom-call | flops 2348810240 | bytes 22020096 | tf_op jit(solution)/shard_map/experts/pallas_call | solution.py:249
  81.2 7.1 %reduce-scatter.2.cloned.1.call-done = f32[128,144]{0,1:T(8,128)} async-done(((f32[1024,144]{0,1:T(8,128)}), f32[128,144]{0,1:T(8,128)}) %reduce-scatter.2.cloned.1.call-update) | async-done | bytes 73744 | tf_op jit(solution)/shard_map/reduce_scatter | solution.py:428
  88.2 1.5 %convert_element_type.81 = bf16[128,144]{0,1:T(8,128)(2,1)} convert(f32[128,144]{0,1:T(8,128)} %reduce-scatter.2.cloned.1.call-done) | non-fusion elementwise | flops 18432 | bytes 110592 | tf_op jit(solution)/shard_map/convert_element_type | solution.py:430
  89.7 1.0 fusion.60
  90.7 0.8 convert_reduce_fusion.1
  91.6 0.6 select_reduce_fusion
  92.4 1.1 %convolution_convert_fusion.2 = bf16[128,1792]{1,0:T(8,128)(2,1)} fusion(bf16[64,1792]{1,0:T(8,128)(2,1)S(1)} %maximum_bitcast_fusion, bf16[128,64]{0,1:T(8,128)(2,1)S(1)} %fusion.36, bf16[128,64]{0,1:T(8,128)(2,1)S(1)} %fusion.35), kind=kOutput, calls=%fused_computation.5 | convolution fusion | flops 59932672 | bytes 720896 | tf_op jit(solution)/shard_map/dot_general | solution.py:318
  (45 shorter events, 1.3 us)
Async XLA Ops:
  7.2 2.8 %copy-start.8 = (bf16[128,576]{0,1:T(8,128)(2,1)S(1)}, bf16[128,576]{0,1:T(8,128)(2,1)}, u32[]{:S(2)}) copy-start(bf16[128,576]{0,1:T(8,128)(2,1)} %param.20) | copy-start | bytes 442372
  7.2 44.2 %all-gather.3.cloned.1.call-start = ((), (), s32[]{:S(2)}) async-start(), calls=%async_computation.2 | async-start | bytes 2293760 | tf_op jit(solution)/shard_map/all_gather | solution.py:425
  8.2 20.1 %copy-start = (bf16[512,1024]{1,0:T(8,128)(2,1)S(1)}, bf16[512,1024]{1,0:T(8,128)(2,1)}, u32[]{:S(2)}) copy-start(bf16[512,1024]{1,0:T(8,128)(2,1)} %param.23) | copy-start | bytes 3145732
  8.3 20.1 %copy-start.1 = (bf16[512,1024]{1,0:T(8,128)(2,1)S(1)}, bf16[512,1024]{1,0:T(8,128)(2,1)}, u32[]{:S(2)}) copy-start(bf16[512,1024]{1,0:T(8,128)(2,1)} %param.24) | copy-start | bytes 3145732
  27.4 60.8 %reduce-scatter.2.cloned.1.call-start = ((), (), s32[]{:S(2)}) async-start(), calls=%async_computation.1 | async-start | bytes 663552 | tf_op jit(solution)/shard_map/reduce_scatter | solution.py:428
  30.0 1.3 %copy-start.3 = (bf16[256,1536]{1,0:T(8,128)(2,1)S(1)}, bf16[256,1536]{1,0:T(8,128)(2,1)}, u32[]{:S(2)}) copy-start(bf16[256,1536]{1,0:T(8,128)(2,1)} %param.21) | copy-start | bytes 2359300
  30.0 1.5 %copy-start.5 = (bf16[256,1024]{1,0:T(8,128)(2,1)S(1)}, bf16[256,1024]{1,0:T(8,128)(2,1)}, u32[]{:S(2)}) copy-start(bf16[256,1024]{1,0:T(8,128)(2,1)} %param.22) | copy-start | bytes 1572868
  30.1 1.7 %copy-start.10 = (s32[256]{0:T(256)S(1)}, s32[256]{0:T(256)}, u32[]{:S(2)}) copy-start(s32[256]{0:T(256)} %param.25) | copy-start | bytes 3076
  31.6 3.8 %copy-start.4 = (bf16[256,1536]{0,1:T(8,128)(2,1)}, bf16[256,1536]{0,1:T(8,128)(2,1)S(1)}, u32[]{:S(2)}) copy-start(bf16[256,1536]{0,1:T(8,128)(2,1)S(1)} %copy.64) | copy-start | bytes 2359300
  31.9 3.4 %copy-start.6 = (bf16[256,8,64]{0,2,1:T(8,128)(2,1)}, bf16[256,8,64]{0,2,1:T(8,128)(2,1)S(1)}, u32[]{:S(2)}) copy-start(bf16[256,8,64]{0,2,1:T(8,128)(2,1)S(1)} %broadcast_in_dim.96) | copy-start | bytes 786436
  42.4 1.9 %copy-start.12 = (f32[8,256,256]{1,2,0:T(8,128)S(1)}, f32[8,256,256]{1,2,0:T(8,128)}, u32[]{:S(2)}) copy-start(f32[8,256,256]{1,2,0:T(8,128)} %get-tuple-element.43) | copy-start | bytes 6291460
  44.3 1.2 %copy-start.2 = (bf16[512,1024]{1,0:T(8,128)(2,1)S(1)}, bf16[512,1024]{1,0:T(8,128)(2,1)}, u32[]{:S(2)}) copy-start(bf16[512,1024]{1,0:T(8,128)(2,1)} %param.24) | copy-start | bytes 3145732
  46.6 1.5 %copy-start.7 = (bf16[256,8,64]{0,2,1:T(8,128)(2,1)S(1)}, bf16[256,8,64]{0,2,1:T(8,128)(2,1)}, u32[]{:S(2)}) copy-start(bf16[256,8,64]{0,2,1:T(8,128)(2,1)} %copy-done.6) | copy-start | bytes 786436
  52.5 39.1 %copy-start.9 = (s32[128,8]{0,1:T(8,128)S(1)}, s32[128,8]{0,1:T(8,128)}, u32[]{:S(2)}) copy-start(s32[128,8]{0,1:T(8,128)} %param.15) | copy-start | bytes 12292
  52.5 39.1 %copy-start.11 = (f32[128,8]{0,1:T(8,128)S(1)}, f32[128,8]{0,1:T(8,128)}, u32[]{:S(2)}) copy-start(f32[128,8]{0,1:T(8,128)} %param.16) | copy-start | bytes 12292
Sparse Core Ops, SparseCore 0:
  27.5 22.5 all-gather.2
  53.3 34.9 reduce-scatter.1
